TPU v7x, 256 devices: a whole 4x4x8 slice. The times are simulated.
256 devices in a mesh: region: 64 (over z, y, core), mp: 4 (over x).
Axes of the slice: x: 4, y: 4, z: 8, core: 2. Of those that a mesh axis runs over, the one named last changes fastest.
Arguments:
- grid_state: bfloat16 [524288, 268], P(('region', 'mp')), may hold values from -6 to 6
- targets: int32 [524288], P(('region', 'mp')), may hold values from 0 to 40959, as said below
- neighbours: int32 [40960, 32], P('region'), may hold values from 0 to 40959, as said below
- w_in: bfloat16 [268, 512], replicated, may hold values from -0.375 to 0.375
- b_in: float32 [512], replicated, may hold values from -0.5 to 0.5
- mesh_gain: float32 [512], replicated, may hold values from 1 to 2
- w_qkv: bfloat16 [3, 512, 512], P(None, None, 'mp'), may hold values from -0.25 to 0.25
- w_out: bfloat16 [512, 512], P('mp'), may hold values from -0.25 to 0.25
- w_dec: bfloat16 [512, 512], replicated, may hold values from -0.25 to 0.25
- w_head: bfloat16 [512, 84], replicated, may hold values from -0.25 to 0.25
Outputs:
- denoised: float32 [524288, 84], P(('region', 'mp'))
Inputs may be any that keep to these rules, and one draw needn't show every extreme that they name: `targets`: the mesh node of a grid point of region r (rows r * 2048 * 4 onward) belongs to region r or r + 1 cyclically; region r owns nodes r * 640 onward. `neighbours`: every neighbour of a node of region r belongs to region r - 1, r or r + 1 cyclically.
All inputs are finite; a program needn't handle non-finite values.
Results may differ from a plain program's by a relative error of at most 0.022.
Values may be sent and summed in bfloat16 or wider, within the bound.
A program may use at most 64 MiB of HBM per device.

v0:
```python
import math

import jax
import jax.numpy as jnp
from jax import lax
from jax.sharding import PartitionSpec as P

HEAD_WIDTH = 128


def passed_along(x, axis, by):
    size = lax.axis_size(axis)
    return lax.ppermute(x, axis, [(i, (i + by) % size) for i in range(size)])


def extended(block, sides, width):
    for axis, dim in sides:
        count = lax.axis_size(axis)
        forward = [(i, i + 1) for i in range(count - 1)]
        forward.append((count - 1, 0))
        backward = [(target, source) for source, target in forward]
        low = lax.ppermute(
            lax.slice_in_dim(block, block.shape[dim] - width, None, axis=dim), axis, forward
        )
        high = lax.ppermute(lax.slice_in_dim(block, 0, width, axis=dim), axis, backward)
        block = jnp.concatenate([low, block, high], axis=dim)
    return block


def carry_next(block):
    return passed_along(block.astype(jnp.bfloat16), "region", 1).astype(block.dtype)


def normalise(mesh_in, mesh_gain):
    return (
        mesh_in * lax.rsqrt(jnp.mean(mesh_in * mesh_in, axis=-1, keepdims=True) + 1e-05) * mesh_gain
    ).astype(jnp.bfloat16)


def on_device(grid_state, targets, neighbours, w_in, b_in, mesh_gain, w_qkv, w_out, w_dec, w_head):
    nodes = neighbours.shape[0]
    regions = lax.axis_size("region")
    here = lax.axis_index("region")
    width = w_in.shape[1]
    local_width = w_qkv.shape[2]
    local_heads = local_width // HEAD_WIDTH
    embed = jax.nn.silu(
        jnp.dot(grid_state, w_in, preferred_element_type=jnp.float32) + b_in
    ).astype(jnp.bfloat16)
    relative = jnp.mod(targets - here * nodes, regions * nodes)
    columns = jnp.arange(2 * nodes, dtype=jnp.int32)
    onehot_picker = (relative[:, None] == columns[None, :]).astype(jnp.bfloat16)
    partial_sums = lax.dot_general(
        onehot_picker, embed, (((0,), (0,)), ((), ())), preferred_element_type=jnp.float32
    )
    partial_sums = partial_sums.reshape(2, nodes, width)
    summed = lax.psum(partial_sums.astype(jnp.bfloat16), "mp").astype(jnp.float32)
    state = normalise(summed[0] + carry_next(summed[1]), mesh_gain)
    query = jnp.dot(state, w_qkv[0], preferred_element_type=jnp.float32).astype(jnp.bfloat16)
    keys = jnp.dot(state, w_qkv[1], preferred_element_type=jnp.float32).astype(jnp.bfloat16)
    values = jnp.dot(state, w_qkv[2], preferred_element_type=jnp.float32).astype(jnp.bfloat16)
    joined = jnp.concatenate([keys, values], axis=1)
    window = extended(joined, (("region", 0),), nodes)
    keys_near = window[:, :local_width]
    values_near = window[:, local_width:]
    span = keys_near.shape[0]
    slot = jnp.mod(neighbours // nodes - here + 1, regions) * nodes + neighbours % nodes
    key_lookup_rows = keys_near.reshape(span, local_heads, HEAD_WIDTH)
    value_lookup_rows = values_near.reshape(span, local_heads, HEAD_WIDTH)
    query_rows = query.reshape(nodes, local_heads, HEAD_WIDTH)
    block_rows = math.gcd(nodes, 128)
    positions = jnp.arange(span, dtype=jnp.int32)
    scale_factor = 1.0 / jnp.sqrt(jnp.float32(HEAD_WIDTH))

    def attend(index):
        start = index * block_rows
        query_tile_rows = lax.dynamic_slice_in_dim(query_rows, start, block_rows, 0)
        slot_block = lax.dynamic_slice_in_dim(slot, start, block_rows, 0)
        counts = jnp.sum(
            (slot_block[:, :, None] == positions[None, None, :]).astype(jnp.float32), axis=1
        )
        present = (counts > 0.0)[:, None, :]
        dense_scores = (
            jnp.einsum(
                "eac,jac->eaj", query_tile_rows, key_lookup_rows, preferred_element_type=jnp.float32
            )
            * scale_factor
        )
        top = jnp.max(jnp.where(present, dense_scores, -1e30), axis=-1, keepdims=True)
        raised = jnp.exp(jnp.where(present, dense_scores - top, -1e30)) * counts[:, None, :]
        weights = (raised / jnp.sum(raised, axis=-1, keepdims=True)).astype(jnp.bfloat16)
        heads_combined = jnp.einsum(
            "eaj,jac->eac", weights, value_lookup_rows, preferred_element_type=jnp.float32
        )
        return heads_combined.astype(jnp.bfloat16).reshape(block_rows, local_width)

    mixed_heads_output = lax.map(attend, jnp.arange(nodes // block_rows, dtype=jnp.int32)).reshape(
        nodes, local_width
    )
    attended = lax.psum(
        jnp.dot(mixed_heads_output, w_out, preferred_element_type=jnp.float32).astype(jnp.bfloat16),
        "mp",
    ).astype(jnp.float32)
    mesh_out = (state.astype(jnp.float32) + attended).astype(jnp.bfloat16)
    following = passed_along(mesh_out, "region", -1)
    both_blocks = jnp.concatenate([mesh_out, following], axis=0)
    looked_up = jnp.dot(onehot_picker, both_blocks, preferred_element_type=jnp.float32)
    dec_in = (looked_up + embed.astype(jnp.float32)).astype(jnp.bfloat16)
    hidden = jax.nn.silu(jnp.dot(dec_in, w_dec, preferred_element_type=jnp.float32)).astype(
        jnp.bfloat16
    )
    return jnp.dot(hidden, w_head, preferred_element_type=jnp.float32)


def solution(mesh):
    placed = (
        P(("region", "mp"), None),
        P(("region", "mp")),
        P("region", None),
        P(),
        P(),
        P(),
        P(None, None, "mp"),
        P("mp", None),
        P(),
        P(),
    )
    return jax.shard_map(
        on_device, mesh=mesh, in_specs=placed, out_specs=P(("region", "mp"), None), check_vma=False
    )
```

profile of v0, /device:TPU:2, one launch (start us, length us, event | category | flops | bytes accessed | tf_op | source)
XLA Modules:
  0.0 225.9 jit_solution(16579197979254545661)
XLA Ops:
  6.5 0.8 add_select_fusion.3
  7.3 0.5 copy-done
  7.8 2.9 %multiply_convert_fusion.1 = bf16[2048,512]{1,0:T(8,128)(2,1)S(1)} fusion(bf16[2048,268]{0,1:T(8,128)(2,1)S(1)} %copy-done, bf16[268,512]{1,0:T(8,128)(2,1)} %param.15, f32[512]{0:T(512)} %param.16), kind=kOutput, calls=%fused_computation.27 | convolution fusion | flops 568328192 | bytes 3471360 | tf_op jit(solution)/shard_map/dot_general | solution.py:48
  10.7 4.4 %fusion.16 = bf16[1280,512]{1,0:T(8,128)(2,1)} fusion(bf16[2048,512]{1,0:T(8,128)(2,1)S(1)} %multiply_convert_fusion.1, s32[2048]{0:T(1024)S(1)} %add_select_fusion.3), kind=kOutput, calls=%fused_computation.28 | convolution fusion | flops 2687631360 | bytes 3416064 | tf_op jit(solution)/shard_map/dot_general | solution.py:53
  15.1 0.0 all-reduce.3.cloned.1.call-update
  15.1 0.0 all-reduce.5.cloned.1.call-start
  15.2 55.1 %all-reduce.3.cloned.1.call-done = bf16[2,640,512]{2,1,0:T(8,128)(2,1)} async-done(((bf16[2,640,512]{2,1,0:T(8,128)(2,1)}), bf16[2,640,512]{2,1,0:T(8,128)(2,1)}) %all-reduce.3.cloned.1.call-update) | async-done | bytes 1310736 | tf_op jit(solution)/shard_map/psum | solution.py:57
  70.3 2.1 slice_bitcast_fusion
  72.3 0.2 copy.22
  72.5 13.4 %collective-permute-done = bf16[640,512]{1,0:T(8,128)(2,1)S(1)} collective-permute-done((bf16[640,512]{1,0:T(8,128)(2,1)}, bf16[640,512]{1,0:T(8,128)(2,1)S(1)}, u32[]{:S(2)}, u32[]{:S(2)}) %collective-permute-start) | collective-permute-done | bytes 655392 | tf_op jit(solution)/shard_map/ppermute | solution.py:13
  85.9 0.3 multiply_reduce_fusion
  86.2 0.6 copy-done.2
  86.7 1.3 multiply_convert_fusion.3
  88.1 0.3 convolution_convert_fusion.2
  88.4 0.3 convolution_convert_fusion.3
  88.8 0.1 collective-permute-start.2
  88.9 0.5 collective-permute-start.1
  89.4 0.5 fusion.29
  89.9 0.3 fusion.24
  90.2 3.3 %collective-permute-done.2 = bf16[640,256]{0,1:T(8,128)(2,1)S(1)} collective-permute-done((bf16[640,256]{0,1:T(8,128)(2,1)S(1)}, bf16[640,256]{0,1:T(8,128)(2,1)S(1)}, u32[]{:S(2)}, u32[]{:S(2)}) %collective-permute-start.2) | collective-permute-done | bytes 327712 | tf_op jit(solution)/shard_map/ppermute | solution.py:25
  93.5 5.5 %collective-permute-done.1 = bf16[640,256]{0,1:T(8,128)(2,1)S(1)} collective-permute-done((bf16[640,256]{0,1:T(8,128)(2,1)S(1)}, bf16[640,256]{0,1:T(8,128)(2,1)S(1)}, u32[]{:S(2)}, u32[]{:S(2)}) %collective-permute-start.1) | collective-permute-done | bytes 327712 | tf_op jit(solution)/shard_map/ppermute | solution.py:22
  99.0 0.1 pad_maximum_fusion
  99.1 0.1 slice_bitcast_fusion.2
  99.1 1.0 copy.26
  100.1 0.3 copy.25
  100.4 44.8 %while.11 = (s32[]{:T(128)}, bf16[5,128,128]{2,1,0:T(8,128)(2,1)S(1)}, s32[5]{0:T(128)S(1)}, s32[640,32]{1,0:T(8,128)S(1)}, bf16[640,1,128]{2,0,1:T(8,128)(2,1)S...) while((s32[]{:T(128)}, ...), condition=%wide.region_6.7_spmd.clone, body=%wide.region_2.6_spmd.clone.sunk | while | flops 152878848 | bytes 9947863 | solution.py:97
  100.5 0.6 dynamic_slice.25
  101.6 6.3 %convert_reduce_fusion.2 = f32[128,1920]{1,0:T(8,128)S(1)} fusion(s32[128,32]{1,0:T(8,128)S(1)} %constant_dynamic-slice_fusion.2), kind=kLoop, calls=%fused_computation.2.clone.1 | loop fusion | flops 23347200 | bytes 999424 | tf_op jit(solution)/shard_map/while/body/eval_jaxpr/reduce_sum | solution.py:79
  107.9 0.4 select_reduce_fusion.2
  108.3 0.4 fusion.56
  108.7 0.2 copy-done.3
  108.9 0.5 fusion.57
  109.4 0.6 dynamic_slice.25
  110.6 6.3 %convert_reduce_fusion.2 = f32[128,1920]{1,0:T(8,128)S(1)} fusion(s32[128,32]{1,0:T(8,128)S(1)} %constant_dynamic-slice_fusion.2), kind=kLoop, calls=%fused_computation.2.clone.1 | loop fusion | flops 23347200 | bytes 999424 | tf_op jit(solution)/shard_map/while/body/eval_jaxpr/reduce_sum | solution.py:79
  116.9 0.4 select_reduce_fusion.2
  117.3 0.4 fusion.56
  117.7 0.2 copy-done.3
  117.9 0.5 fusion.57
  118.4 0.6 dynamic_slice.25
  119.5 6.3 %convert_reduce_fusion.2 = f32[128,1920]{1,0:T(8,128)S(1)} fusion(s32[128,32]{1,0:T(8,128)S(1)} %constant_dynamic-slice_fusion.2), kind=kLoop, calls=%fused_computation.2.clone.1 | loop fusion | flops 23347200 | bytes 999424 | tf_op jit(solution)/shard_map/while/body/eval_jaxpr/reduce_sum | solution.py:79
  125.8 0.4 select_reduce_fusion.2
  126.2 0.4 fusion.56
  126.6 0.2 copy-done.3
  126.9 0.5 fusion.57
  127.3 0.6 dynamic_slice.25
  128.5 6.3 %convert_reduce_fusion.2 = f32[128,1920]{1,0:T(8,128)S(1)} fusion(s32[128,32]{1,0:T(8,128)S(1)} %constant_dynamic-slice_fusion.2), kind=kLoop, calls=%fused_computation.2.clone.1 | loop fusion | flops 23347200 | bytes 999424 | tf_op jit(solution)/shard_map/while/body/eval_jaxpr/reduce_sum | solution.py:79
  134.8 0.4 select_reduce_fusion.2
  135.2 0.4 fusion.56
  135.6 0.2 copy-done.3
  135.8 0.5 fusion.57
  136.3 0.6 dynamic_slice.25
  137.5 6.3 %convert_reduce_fusion.2 = f32[128,1920]{1,0:T(8,128)S(1)} fusion(s32[128,32]{1,0:T(8,128)S(1)} %constant_dynamic-slice_fusion.2), kind=kLoop, calls=%fused_computation.2.clone.1 | loop fusion | flops 23347200 | bytes 999424 | tf_op jit(solution)/shard_map/while/body/eval_jaxpr/reduce_sum | solution.py:79
  143.8 0.4 select_reduce_fusion.2
  144.2 0.4 fusion.56
  144.5 0.2 copy-done.3
  144.8 0.5 fusion.57
  145.3 1.2 convolution_convert_fusion.1
  146.4 0.0 all-reduce.5.cloned.1.call-update
  146.4 47.1 %all-reduce.5.cloned.1.call-done = bf16[640,512]{1,0:T(8,128)(2,1)} async-done(((bf16[640,512]{1,0:T(8,128)(2,1)}), bf16[640,512]{1,0:T(8,128)(2,1)}) %all-reduce.5.cloned.1.call-update) | async-done | bytes 655376 | tf_op jit(solution)/shard_map/psum | solution.py:100
  193.6 1.3 add_convert_fusion.1
  194.9 4.0 %collective-permute-start.3 = (bf16[640,512]{1,0:T(8,128)(2,1)S(1)}, bf16[640,512]{1,0:T(8,128)(2,1)S(1)}, u32[]{:S(2)}, u32[]{:S(2)}) collective-permute-start(bf16[640,512]{1,0:T(8,128)(2,1)S(1)} %add_convert_fusion.1), channel_id=1, source_target_pairs={{0,252},{4,0},{8,4},{12,8},{16,12},{20,16},{24,20},{28,24},{32,28}... | collective-permute-start | bytes 1966088 | tf_op jit(solution)/shard_map/ppermute | solution.py:13
  198.8 8.1 %collective-permute-done.3 = bf16[640,512]{1,0:T(8,128)(2,1)S(1)} collective-permute-done((bf16[640,512]{1,0:T(8,128)(2,1)S(1)}, bf16[640,512]{1,0:T(8,128)(2,1)S(1)}, u32[]{:S(2)}, u32[]{:S(2)}) %collective-permute-start.3) | collective-permute-done | bytes 655392 | tf_op jit(solution)/shard_map/ppermute | solution.py:13
  207.0 7.7 %fusion.22 = f32[2048,512]{1,0:T(8,128)} fusion(bf16[512,512]{1,0:T(8,128)(2,1)S(1)} %copy-done.9, bf16[2048,512]{1,0:T(8,128)(2,1)} %copy-done.11, s32[2048]{0:T(1024)S(1)} %add_select_fusion.3, bf16[640,512]{1,0:T(8,128)(2,1)S(1)} %collective-permute-done.3, bf16[640,512]{1,0:T(8,128)(2,1)S(1)} %add_convert_fusion.1), kind=kOutput, calls=%fused_computation.41 | convolution fusion | flops 3766484992 | bytes 8134656 | tf_op jit(solution)/shard_map/dot_general | solution.py:109
  214.7 4.4 %fusion.17 = f32[2048,84]{0,1:T(8,128)} fusion(bf16[512,84]{0,1:T(8,128)(2,1)S(1)} %copy-done.10, f32[2048,512]{1,0:T(8,128)} %fusion.22), kind=kOutput, calls=%fused_computation.29 | convolution fusion | flops 181403648 | bytes 4968448 | tf_op jit(solution)/shard_map/dot_general | solution.py:112
  (36 shorter events, 0.2 us)
Async XLA Ops:
  6.5 1.3 copy-start
  6.5 63.7 %all-reduce.3.cloned.1.call-start = ((), (), s32[]{:S(2)}) async-start(), calls=%async_computation | async-start | bytes 2621440 | tf_op jit(solution)/shard_map/psum | solution.py:57
  10.7 4.4 %copy-start.11 = (bf16[2048,512]{1,0:T(8,128)(2,1)}, bf16[2048,512]{1,0:T(8,128)(2,1)S(1)}, u32[]{:S(2)}) copy-start(bf16[2048,512]{1,0:T(8,128)(2,1)S(1)} %multiply_convert_fusion.1) | copy-start | bytes 6291460
  15.1 57.2 %copy-start.7 = (s32[640,32]{0,1:T(8,128)S(1)}, s32[640,32]{0,1:T(8,128)}, u32[]{:S(2)}) copy-start(s32[640,32]{0,1:T(8,128)} %param.14) | copy-start | bytes 245764
  15.1 71.6 %copy-start.8 = (f32[512]{0:T(512)S(1)}, f32[512]{0:T(512)}, u32[]{:S(2)}) copy-start(f32[512]{0:T(512)} %param.17) | copy-start | bytes 6148
  15.1 178.5 %all-reduce.5.cloned.1.call-start = ((), (), s32[]{:S(2)}) async-start(), calls=%async_computation.1 | async-start | bytes 1310720 | tf_op jit(solution)/shard_map/psum | solution.py:100
  70.3 15.6 %copy-start.1 = (bf16[2,640,512]{2,1,0:T(8,128)(2,1)S(1)}, bf16[2,640,512]{2,1,0:T(8,128)(2,1)}, u32[]{:S(2)}) copy-start(bf16[2,640,512]{2,1,0:T(8,128)(2,1)} %all-reduce.3.cloned.1.call-done) | copy-start | bytes 3932164
  72.3 13.5 %collective-permute-start = (bf16[640,512]{1,0:T(8,128)(2,1)}, bf16[640,512]{1,0:T(8,128)(2,1)S(1)}, u32[]{:S(2)}, u32[]{:S(2)}) collective-permute-start(bf16[640,512]{1,0:T(8,128)(2,1)} %slice_bitcast_fusion), channel_id=1, source_target_pairs={{0,4},{4,8},{8,12},{12,16},{16,20},{20,24},{24,28},{28,32},{32,36}... | collective-permute-start | bytes 1966088 | tf_op jit(solution)/shard_map/ppermute | solution.py:13
  72.5 15.6 %copy-start.4 = (bf16[3,512,128]{2,1,0:T(8,128)(2,1)S(1)}, bf16[3,512,128]{2,1,0:T(8,128)(2,1)}, u32[]{:S(2)}) copy-start(bf16[3,512,128]{2,1,0:T(8,128)(2,1)} %param.18) | copy-start | bytes 1179652
  85.9 0.8 copy-start.2
  88.8 4.7 %collective-permute-start.2 = (bf16[640,256]{0,1:T(8,128)(2,1)S(1)}, bf16[640,256]{0,1:T(8,128)(2,1)S(1)}, u32[]{:S(2)}, u32[]{:S(2)}) collective-permute-start(bf16[640,256]{0,1:T(8,128)(2,1)S(1)} %pad_maximum_fusion.1), channel_id=1, source_target_pairs={{4,0},{8,4},{12,8},{16,12},{20,16},{24,20},{28,24},{32,28},{36,32}... | collective-permute-start | bytes 983048 | tf_op jit(solution)/shard_map/ppermute | solution.py:25
  88.9 10.1 %collective-permute-start.1 = (bf16[640,256]{0,1:T(8,128)(2,1)S(1)}, bf16[640,256]{0,1:T(8,128)(2,1)S(1)}, u32[]{:S(2)}, u32[]{:S(2)}) collective-permute-start(bf16[640,256]{0,1:T(8,128)(2,1)S(1)} %pad_maximum_fusion.1), channel_id=1, source_target_pairs={{0,4},{4,8},{8,12},{12,16},{16,20},{20,24},{24,28},{28,32},{32,36}... | collective-permute-start | bytes 983048 | tf_op jit(solution)/shard_map/ppermute | solution.py:22
  99.1 1.4 copy-start.5
  100.4 44.8 %copy-start.6 = (bf16[128,512]{1,0:T(8,128)(2,1)S(1)}, bf16[128,512]{1,0:T(8,128)(2,1)}, u32[]{:S(2)}) copy-start(bf16[128,512]{1,0:T(8,128)(2,1)} %param.19) | copy-start | bytes 393220
  107.9 1.0 copy-start.3
  116.9 1.0 copy-start.3
  125.8 1.0 copy-start.3
  134.8 1.0 copy-start.3
  143.7 1.0 copy-start.3
  145.2 61.7 %copy-start.9 = (bf16[512,512]{1,0:T(8,128)(2,1)S(1)}, bf16[512,512]{1,0:T(8,128)(2,1)}, u32[]{:S(2)}) copy-start(bf16[512,512]{1,0:T(8,128)(2,1)} %param.20) | copy-start | bytes 1572868
  194.8 19.8 %copy-start.10 = (bf16[512,84]{0,1:T(8,128)(2,1)S(1)}, bf16[512,84]{0,1:T(8,128)(2,1)}, u32[]{:S(2)}) copy-start(bf16[512,84]{0,1:T(8,128)(2,1)} %param.21) | copy-start | bytes 258052
  194.9 12.1 %collective-permute-start.3 = (bf16[640,512]{1,0:T(8,128)(2,1)S(1)}, bf16[640,512]{1,0:T(8,128)(2,1)S(1)}, u32[]{:S(2)}, u32[]{:S(2)}) collective-permute-start(bf16[640,512]{1,0:T(8,128)(2,1)S(1)} %add_convert_fusion.1), channel_id=1, source_target_pairs={{0,252},{4,0},{8,4},{12,8},{16,12},{20,16},{24,20},{28,24},{32,28}... | collective-permute-start | bytes 1966088 | tf_op jit(solution)/shard_map/ppermute | solution.py:13
Sparse Core Ops, SparseCore 0:
  15.3 54.9 all-reduce.2
  146.6 46.9 all-reduce.4
where the time goes:
time: 226 us
  waiting for transfers between devices  132 us (58%)
  other arithmetic  37.6 us (17%)
  matrix products  25.8 us (11%)
  between operations  13.6 us (6%)
  local copies, waits for them, and re-layouts  8.78 us (4%)
  starting transfers between devices  4.62 us (2%)
  loops' own time  3.06 us (1%)
    psum x1, waiting for transfers between devices, on_device(): lax.psum(partial_sums.astype(jnp.bfloat16), 'mp').astype(jnp.float32)  55.1 us
    psum x1, waiting for transfers between devices, on_device(): lax.psum(jnp.dot(mixed_heads_output, w_out, preferred_element_type=jnp.fl...  47.1 us
    reduce_sum x5, other arithmetic, attend(): jnp.sum((slot_block[:, :, None] == positions[None, None, :]).astype(jnp.f...  31.4 us
    ppermute x2, waiting for transfers between devices, passed_along(): return lax.ppermute(x, axis, [(i, (i + by) % size) for i in range(size)])  21.5 us
    dot_general x1, matrix products, on_device(): jnp.dot(dec_in, w_dec, preferred_element_type=jnp.float32)  7.72 us
    ppermute x1, waiting for transfers between devices, extended(): lax.ppermute(lax.slice_in_dim(block, block.shape[dim] - width, None, axis...  5.49 us
  transfers between devices with their start and end apart: 6, of which 6 were waited for; matrix products, arithmetic and copies ran while one was open for 0% of the time, Pallas kernels for 0%

commit v1 on v0

v1 whole, which is shorter than its diff:
```python
import functools

import jax
import jax.numpy as jnp
from jax import lax
from jax.experimental import pallas as pl
from jax.experimental.pallas import tpu as pltpu
from jax.sharding import PartitionSpec as P

MESH = pl.DeviceIdType.MESH
BF16 = jnp.bfloat16
F32 = jnp.float32
LOG2_E = 1.4426950408889634
ABSENT = -1e30

NAMES = (
    *("wr", "wl", "w2r", "w2l", "ws0", "ws1", "ws2", "ws3"),
    *("or", "ol", "o2r", "o2l", "os0", "os1", "os2", "os3"),
    *("n0", "n1", "n2", "n3"),
    *("ar", "al", "br0", "br1", "bl0", "bl1"),
    *("sr", "sl", "s2r", "s2l"),
    *("su0", "su1", "su2", "su3", "su4", "sd0", "sd1", "sd2", "sd3", "sd4"),
    *("mr", "ml", "m2r", "m2l", "md0", "md1", "md2", "md3", "md4"),
)
INDEX = {name: i for i, name in enumerate(NAMES)}


def nt(a, b):
    return lax.dot_general(a, b, (((1,), (1,)), ((), ())), preferred_element_type=F32)


def nn(a, b):
    return jnp.dot(a, b, preferred_element_type=F32)


def silu(z):
    half = 0.5 * z
    return half + half * jnp.tanh(half)


def kernel(
    regions,
    x_hbm, targets_ref, nbr_ref, w_in_hbm, b_ref, gain_ref, wqkv_hbm, wo_hbm, wdec_hbm, whead_hbm,
    out_ref,
    x, w_in, w_in_t, b_t, wqkv, wo, wdec, wdec_t, whead,
    rel, slots, onehot, embed, e2, send_n, recv_n, part, ra, ra_l, ra_r, rb, rb_l, rb_r,
    st, qp, bias, mix, md, md_t,
    ssem, rsem, lsem,
):
    r = lax.axis_index("region")
    m = lax.axis_index("mp")
    mps = 4
    up = (lax.rem(r + 1, regions), m)
    down = (lax.rem(r + regions - 1, regions), m)
    right_m = lax.rem(m + 1, mps)
    left_m = lax.rem(m + mps - 1, mps)
    opp_m = lax.rem(m + 2, mps)
    right = (r, right_m)
    left = (r, left_m)
    core = lax.rem(r, 2)
    sibling = (r + 1 - 2 * core, m)

    channels, points = x.shape
    width = embed.shape[0]
    quarter = st.shape[0] // 12
    nodes = 4 * quarter
    half = quarter // 2
    neighbours = slots.shape[1]
    heads, head_width = wo.shape[0], wo.shape[1]
    block = min(256, points)
    blocks = points // block

    started = []

    def copy(name, src, dst, dev):
        i = INDEX[name]
        return pltpu.make_async_remote_copy(
            src_ref=src, dst_ref=dst, send_sem=ssem.at[i], recv_sem=rsem.at[i],
            device_id=dev, device_id_type=MESH,
        )

    def send(name, src, dst, dev):
        c = copy(name, src, dst, dev)
        c.start()
        started.append(c)

    def arrived(name, dst):
        copy(name, dst, dst, right).wait_recv()

    loads = {}
    for i, (name, src, dst) in enumerate((
        ("w_in", w_in_hbm, w_in), ("x", x_hbm, x), ("wqkv", wqkv_hbm, wqkv.at[m]),
        ("wo", wo_hbm, wo.at[m]), ("wdec", wdec_hbm, wdec), ("whead", whead_hbm, whead),
    )):
        loads[name] = pltpu.make_async_copy(src, dst, lsem.at[i])
        loads[name].start()

    barrier = pltpu.get_barrier_semaphore()
    for dev in (up, down, right, left):
        pl.semaphore_signal(barrier, inc=1, device_id=dev, device_id_type=MESH)

    here = r * nodes
    total = regions * nodes
    t = targets_ref[...] - here
    rel[...] = jnp.where(t < 0, t + total, t)
    b_t[...] = jnp.transpose(jnp.broadcast_to(b_ref[...], (128, width)))
    loads["w_in"].wait()
    w_in_t[...] = jnp.transpose(w_in[...].astype(F32)).astype(BF16)

    pl.semaphore_wait(barrier, 4)

    hq = width // 2
    ho = head_width // 2

    def qkv_part(h, start, size):
        return wqkv.at[h, :, pl.ds(pl.multiple_of(start, 16), size), :]

    def wo_part(h, start, size):
        return wo.at[h, pl.ds(pl.multiple_of(start, 16), size), :]

    q0, o0 = core * hq, core * ho
    loads["wqkv"].wait()
    loads["wo"].wait()
    for name, dev in (("r", right), ("l", left)):
        send("w" + name, qkv_part(m, q0, hq), qkv_part(m, q0, hq), dev)
        send("o" + name, wo_part(m, o0, ho), wo_part(m, o0, ho), dev)

    loads["x"].wait()

    def embed_block(i, _):
        cols = pl.ds(pl.multiple_of(i * block, block), block)
        z = nn(w_in_t[...], x[:, cols]) + jnp.concatenate([b_t[...]] * (block // 128), axis=1)
        embed[:, cols] = silu(z).astype(BF16)
        return 0

    lax.fori_loop(0, blocks, embed_block, 0)

    order = (opp_m, right_m, left_m, m)

    def pick_block(base):
        ids = lax.broadcasted_iota(jnp.int32, (quarter, points), 0) + base
        return (ids == rel[...]).astype(F32).astype(BF16)

    for k in range(4):
        rows = pl.ds(pl.multiple_of(nodes + order[k] * quarter, 16), quarter)
        onehot[rows, :] = pick_block(nodes + order[k] * quarter)
        send_n[k] = nt(onehot[rows, :], embed[...]).astype(BF16)
        send("n%d" % k, send_n.at[k], recv_n.at[k], up)
    for k in range(4):
        rows = pl.ds(pl.multiple_of(order[k] * quarter, 16), quarter)
        onehot[rows, :] = pick_block(order[k] * quarter)
        part[k] = nt(onehot[rows, :], embed[...])

    arrived("wr", qkv_part(m, q0, hq))
    arrived("or", wo_part(m, o0, ho))
    send("w2r", qkv_part(left_m, q0, hq // 2), qkv_part(left_m, q0, hq // 2), right)
    send("o2r", wo_part(left_m, o0, ho // 2), wo_part(left_m, o0, ho // 2), right)
    send("ws0", qkv_part(left_m, q0, hq), qkv_part(left_m, q0, hq), sibling)
    send("os0", wo_part(left_m, o0, ho), wo_part(left_m, o0, ho), sibling)
    arrived("wl", qkv_part(m, q0, hq))
    arrived("ol", wo_part(m, o0, ho))
    send("w2l", qkv_part(right_m, q0 + hq // 2, hq // 2), qkv_part(right_m, q0 + hq // 2, hq // 2), left)
    send("o2l", wo_part(right_m, o0 + ho // 2, ho // 2), wo_part(right_m, o0 + ho // 2, ho // 2), left)
    send("ws1", qkv_part(right_m, q0, hq), qkv_part(right_m, q0, hq), sibling)
    send("os1", wo_part(right_m, o0, ho), wo_part(right_m, o0, ho), sibling)

    lo, hi = pl.ds(0, half), pl.ds(half, half)
    arrived("n0", recv_n.at[0])
    ra[...] = (part[0] + recv_n[0].astype(F32)).astype(BF16)
    send("ar", ra.at[lo], ra_l, right)
    send("al", ra.at[hi], ra_r, left)
    arrived("n1", recv_n.at[1])
    rb[0, hi] = (part[1, hi] + recv_n[1, hi].astype(F32)).astype(BF16)
    send("br1", rb.at[0, hi], rb_l.at[hi], right)
    arrived("n2", recv_n.at[2])
    rb[1, lo] = (part[2, lo] + recv_n[2, lo].astype(F32)).astype(BF16)
    send("bl0", rb.at[1, lo], rb_r.at[lo], left)
    arrived("ar", ra_l)
    rb[0, lo] = (part[1, lo] + recv_n[1, lo].astype(F32) + ra_l[...].astype(F32)).astype(BF16)
    send("br0", rb.at[0, lo], rb_l.at[lo], right)
    arrived("al", ra_r)
    rb[1, hi] = (part[2, hi] + recv_n[2, hi].astype(F32) + ra_r[...].astype(F32)).astype(BF16)
    send("bl1", rb.at[1, hi], rb_r.at[hi], left)
    arrived("n3", recv_n.at[3])

    slots_all = jnp.transpose(nbr_ref[...])
    s = slots_all - (here - nodes)
    s = jnp.where(s < 0, s + total, s)
    slots[...] = jnp.where(s >= total, s - total, s)
    span = 3 * nodes

    def count_block(i, _):
        rows = slots[pl.ds(pl.multiple_of(m * quarter + i * 8, 8), 8), :]
        ids = lax.broadcasted_iota(jnp.int32, (8, span), 1)
        count = jnp.zeros((8, span), F32)
        for k in range(neighbours):
            count = count + (rows[:, k:k + 1] == ids).astype(F32)
        bias[pl.ds(pl.multiple_of(i * 8, 8), 8), :] = jnp.where(count > 0.0, jnp.log2(count), ABSENT)
        return 0

    lax.fori_loop(0, quarter // 8, count_block, 0)

    arrived("w2r", qkv_part(opp_m, q0, hq // 2))
    arrived("o2r", wo_part(opp_m, o0, ho // 2))
    send("ws2", qkv_part(opp_m, q0, hq // 2), qkv_part(opp_m, q0, hq // 2), sibling)
    send("os2", wo_part(opp_m, o0, ho // 2), wo_part(opp_m, o0, ho // 2), sibling)
    arrived("w2l", qkv_part(opp_m, q0, hq // 2))
    arrived("o2l", wo_part(opp_m, o0, ho // 2))
    send("ws3", qkv_part(opp_m, q0 + hq // 2, hq // 2), qkv_part(opp_m, q0 + hq // 2, hq // 2), sibling)
    send("os3", wo_part(opp_m, o0 + ho // 2, ho // 2), wo_part(opp_m, o0 + ho // 2, ho // 2), sibling)

    for name, ref in (("br0", rb_l.at[lo]), ("br1", rb_l.at[hi]), ("bl0", rb_r.at[lo]), ("bl1", rb_r.at[hi])):
        arrived(name, ref)
    mesh_in = part[3] + recv_n[3].astype(F32) + rb_l[...].astype(F32) + rb_r[...].astype(F32)
    mean = jnp.mean(mesh_in * mesh_in, axis=-1, keepdims=True)
    state = (mesh_in * lax.rsqrt(mean + 1e-05) * gain_ref[...]).astype(BF16)

    def rows_of(ref, slot, q, start=0, size=quarter):
        return ref.at[pl.ds(pl.multiple_of(slot * nodes + q * quarter + start, 16), size)]

    own = rows_of(st, 1, m)
    own[...] = state

    def gather_ring(ref, slot, tag):
        send(tag + "r", rows_of(ref, slot, m), rows_of(ref, slot, m), right)
        send(tag + "l", rows_of(ref, slot, m), rows_of(ref, slot, m), left)
        yield 0, (m, 0, quarter)
        arrived(tag + "r", rows_of(ref, slot, left_m))
        send(tag + "2r", rows_of(ref, slot, left_m, 0, half), rows_of(ref, slot, left_m, 0, half), right)
        yield 1, (left_m, 0, quarter)
        arrived(tag + "l", rows_of(ref, slot, right_m))
        send(tag + "2l", rows_of(ref, slot, right_m, half, half), rows_of(ref, slot, right_m, half, half), left)
        yield 2, (right_m, 0, quarter)
        arrived(tag + "2r", rows_of(ref, slot, opp_m, 0, half))
        yield 3, (opp_m, 0, half)
        arrived(tag + "2l", rows_of(ref, slot, opp_m, half, half))
        yield 4, (opp_m, half, half)

    for i, (q, start, size) in gather_ring(st, 1, "s"):
        send("su%d" % i, rows_of(st, 1, q, start, size), rows_of(st, 0, q, start, size), up)
        send("sd%d" % i, rows_of(st, 1, q, start, size), rows_of(st, 2, q, start, size), down)

    for i, h in enumerate((left_m, right_m)):
        arrived("ws%d" % i, qkv_part(h, hq - q0, hq))
        arrived("os%d" % i, wo_part(h, ho - o0, ho))
    for i in (2, 3):
        arrived("ws%d" % i, qkv_part(opp_m, hq - q0, hq // 2))
        arrived("os%d" % i, wo_part(opp_m, ho - o0, ho // 2))
    scale = LOG2_E * head_width ** -0.5
    for h in range(heads):
        q = nn(own[...], wqkv[h, 0]).astype(BF16)
        qp[pl.ds(h * quarter, quarter), :] = (nt(q, wqkv[h, 1]) * scale).astype(BF16)

    loads["wdec"].wait()
    wdec_t[...] = jnp.transpose(wdec[...].astype(F32)).astype(BF16)

    def e2_block(i, _):
        cols = pl.ds(pl.multiple_of(i * block, block), block)
        e2[:, cols] = nn(wdec_t[...], embed[:, cols])
        return 0

    lax.fori_loop(0, blocks, e2_block, 0)

    for i in range(5):
        size = quarter if i < 3 else half
        arrived("su%d" % i, rows_of(st, 0, 0, 0, size))
        arrived("sd%d" % i, rows_of(st, 0, 0, 0, size))

    def attend(h, _):
        rows = pl.ds(pl.multiple_of(h * quarter, 16), quarter)
        sc = nt(qp[rows, :], st[...]) + bias[...]
        top = jnp.max(sc, axis=-1, keepdims=True)
        raised = jnp.exp2(sc - top)
        norm = jnp.sum(raised, axis=-1, keepdims=True)
        mixed = nn(raised.astype(BF16), st[...]) / norm
        v = nn(mixed.astype(BF16), wqkv[h, 2]).astype(BF16)
        mix[...] += nn(v, wo[h])
        return 0

    mix[...] = own[...].astype(F32)
    lax.fori_loop(0, heads, attend, 0)
    mesh_out = mix[...].astype(BF16)
    rows_of(md, 0, m)[...] = nn(mesh_out, wdec[...]).astype(BF16)

    for i, (q, start, size) in gather_ring(md, 0, "m"):
        send("md%d" % i, rows_of(md, 0, q, start, size), rows_of(md, 1, q, start, size), down)

    md_t[...] = jnp.transpose(md[pl.ds(0, nodes), :].astype(F32)).astype(BF16)

    def own_block(i, _):
        cols = pl.ds(pl.multiple_of(i * block, block), block)
        e2[:, cols] += nn(md_t[...], onehot[pl.ds(0, nodes), cols])
        return 0

    lax.fori_loop(0, blocks, own_block, 0)

    loads["whead"].wait()
    for i in range(5):
        size = quarter if i < 3 else half
        arrived("md%d" % i, rows_of(md, 1, 0, 0, size))
    md_t[...] = jnp.transpose(md[pl.ds(nodes, nodes), :].astype(F32)).astype(BF16)

    def last_block(i, _):
        cols = pl.ds(pl.multiple_of(i * block, block), block)
        z = e2[:, cols] + nn(md_t[...], onehot[pl.ds(nodes, nodes), cols])
        out_ref[:, cols] = nn(whead[...], silu(z).astype(BF16))
        return 0

    lax.fori_loop(0, blocks, last_block, 0)

    for c in started:
        c.wait_send()


def on_device(grid_state, targets, neighbours, w_in, b_in, mesh_gain, w_qkv, w_out, w_dec, w_head):
    points, channels = grid_state.shape
    nodes, nbr = neighbours.shape
    width = w_in.shape[1]
    quarter = nodes // 4
    half = quarter // 2
    span = 3 * nodes
    heads = 4
    head_width = w_qkv.shape[2]
    out_width = w_head.shape[1]
    regions = lax.axis_size("region")
    vmem = pl.BlockSpec(memory_space=pltpu.VMEM)
    anyw = pl.BlockSpec(memory_space=pl.ANY)
    V = pltpu.VMEM
    out = pl.pallas_call(
        functools.partial(kernel, regions),
        out_shape=jax.ShapeDtypeStruct((out_width, points), F32),
        in_specs=[anyw, vmem, vmem, anyw, vmem, vmem, anyw, anyw, anyw, anyw],
        out_specs=vmem,
        scratch_shapes=[
            V((channels, points), BF16), V((channels, width), BF16), V((width, channels), BF16),
            V((width, 128), F32), V((heads, 3, width, head_width), BF16), V((heads, head_width, width), BF16),
            V((width, width), BF16), V((width, width), BF16), V((out_width, width), BF16),
            V((1, points), jnp.int32), V((nodes, nbr), jnp.int32), V((2 * nodes, points), BF16),
            V((width, points), BF16), V((width, points), F32),
            V((4, quarter, width), BF16), V((4, quarter, width), BF16), V((4, quarter, width), F32),
            V((quarter, width), BF16), V((half, width), BF16), V((half, width), BF16),
            V((2, quarter, width), BF16), V((quarter, width), BF16), V((quarter, width), BF16),
            V((span, width), BF16), V((heads * quarter, width), BF16), V((quarter, span), F32),
            V((quarter, width), F32), V((2 * nodes, width), BF16), V((width, nodes), BF16),
            pltpu.SemaphoreType.DMA((len(NAMES),)), pltpu.SemaphoreType.DMA((len(NAMES),)),
            pltpu.SemaphoreType.DMA((6,)),
        ],
        compiler_params=pltpu.CompilerParams(
            collective_id=0, has_side_effects=True, vmem_limit_bytes=56 * 1024 * 1024
        ),
        cost_estimate=pl.CostEstimate(flops=10 * 10 ** 9, bytes_accessed=4 * 10 ** 6, transcendentals=3 * 10 ** 6),
    )(
        grid_state.T, targets.reshape(1, points), neighbours.T, w_in, b_in.reshape(1, width),
        mesh_gain.reshape(1, width), w_qkv, w_out, w_dec, w_head.T,
    )
    return out.T


def solution(mesh):
    placed = (
        P(("region", "mp"), None),
        P(("region", "mp")),
        P("region", None),
        P(),
        P(),
        P(),
        P(None, None, "mp"),
        P("mp", None),
        P(),
        P(),
    )
    return jax.shard_map(
        on_device, mesh=mesh, in_specs=placed, out_specs=P(("region", "mp"), None), check_vma=False
    )
```

time: 226 us -> 71.7 us (0.32)
  waiting for transfers between devices: 132 us -> 0 us
  Pallas kernels: 0 us -> 69 us
  other arithmetic: 37.6 us -> 0 us
  matrix products: 25.8 us -> 0 us
  between operations: 13.6 us -> 0.01 us
  local copies, waits for them, and re-layouts: 8.78 us -> 2.02 us
  starting transfers between devices: 4.62 us -> 0 us
  loops' own time: 3.06 us -> 0 us
    psum x2 -> x0, waiting for transfers between devices: 102 us -> none  [the longest x1 55.1 us: on_device(): lax.psum(partial_sums.astype(jnp.bfloat16), 'mp').astype(jnp.float32)]
    pallas_call x0 -> x1, Pallas kernels: none -> 69 us  [on_device(): pl.pallas_call(functools.partial(kernel, regions), out_shape=jax.ShapeDty...]
    reduce_sum x11 -> x0, other arithmetic: 33.6 us -> none  [the longest x5 31.4 us: attend(): jnp.sum((slot_block[:, :, None] == positions[None, None, :]).astype(jnp.f...]
    ppermute x4 -> x0, waiting for transfers between devices: 30.2 us -> none  [the longest x2 21.5 us: passed_along(): return lax.ppermute(x, axis, [(i, (i + by) % size) for i in range(size)])]
    dot_general x18 -> x0, matrix products: 25.8 us -> none  [the longest x1 7.72 us: on_device(): jnp.dot(dec_in, w_dec, preferred_element_type=jnp.float32)]
    ppermute x4 -> x0, starting transfers between devices: 4.57 us -> none  [the longest x2 3.99 us: passed_along(): return lax.ppermute(x, axis, [(i, (i + by) % size) for i in range(size)])]
    another operation x1 -> x0, loops' own time: 3.06 us -> none  [on_device(): lax.map(attend, jnp.arange(nodes // block_rows, dtype=jnp.int32))]
    dynamic_slice x10 -> x0, local copies, waits for them, and re-layouts: 2.96 us -> none  [the longest x5 2.9 us: on_device(): lax.map(attend, jnp.arange(nodes // block_rows, dtype=jnp.int32))]
  transfers between devices with their start and end apart: 6 -> 0, of which waited for: 6 -> 0; matrix products, arithmetic and copies ran while one was open for 0% -> 0% of each run, Pallas kernels for 0% -> 0%
where the time goes in v1:
time: 71.7 us; the launch traced here: 71.1 us
  Pallas kernels  69 us (96%)
  local copies, waits for them, and re-layouts  2.02 us (3%)
    pallas_call x1, Pallas kernels, on_device(): pl.pallas_call(functools.partial(kernel, regions), out_shape=jax.ShapeDty...  69 us
    unnamed x1, local copies, waits for them, and re-layouts  2.02 us

profile of v1, /device:TPU:2, one launch (start us, length us, event | category | flops | bytes accessed | tf_op | source)
XLA Modules:
  0.0 71.1 jit_solution(5557554855519026686)
XLA Ops:
  0.0 69.0 %shard_map.100 = f32[84,2048]{1,0:T(8,128)} custom-call(bf16[268,2048]{1,0:T(8,128)(2,1)} %bitcast.8, s32[1,2048]{1,0:T(1,128)} %bitcast.11, s32[32,640]{1,0:T(8,128)} %bitcast.10, bf16[268,512]{1,0:T(8,128)(2,1)} %w_in_hbm.1, f32[1,512]{1,0:T(1,128)} %bitcast.12, f32[1,512]{1,0:T(1,128)} %bitcast.13, bf16[3,512,128]{2,1,0:T(8,128)(2,1)} %wqkv_hbm.1, ...), custom_call_target="tpu_custom_call" | custom-call | flops 10000000000 | bytes 4000000 | tf_op jit(solution)/shard_map/pallas_call | solution.py:329
  69.1 2.0 %copy.12 = f32[2048,84]{0,1:T(8,128)} copy(f32[2048,84]{0,1:T(8,128)} %bitcast.7) | data formatting | bytes 1376256

commit v2 on v1

v2 whole, which is shorter than its diff:
```python
import functools

import jax
import jax.numpy as jnp
from jax import lax
from jax.experimental import pallas as pl
from jax.experimental.pallas import tpu as pltpu
from jax.sharding import PartitionSpec as P

MESH = pl.DeviceIdType.MESH
BF16 = jnp.bfloat16
F32 = jnp.float32
LOG2_E = 1.4426950408889634
ABSENT = -1e30

NAMES = (
    *("wr", "wl", "w2r", "w2l", "ws0", "ws1", "ws2", "ws3"),
    *("vr", "vl", "v2r", "v2l", "vs0", "vs1", "vs2", "vs3"),
    *("or", "ol", "o2r", "o2l", "os0", "os1", "os2", "os3"),
    *("n0", "n1", "n2", "n3"),
    *("ar", "al", "br0", "br1", "bl0", "bl1"),
    *("sr0", "sr1", "sl0", "sl1", "sf0", "sf1"),
    *("su0", "su1", "su2", "su3", "su4", "su5", "su6"),
    *("sd0", "sd1", "sd2", "sd3", "sd4", "sd5", "sd6"),
    *("mr0", "mr1", "ml0", "ml1", "mf0", "mf1"),
    *("md0", "md1", "md2", "md3", "md4", "md5", "md6"),
)
INDEX = {name: i for i, name in enumerate(NAMES)}


def nt(a, b):
    return lax.dot_general(a, b, (((1,), (1,)), ((), ())), preferred_element_type=F32)


def nn(a, b):
    return jnp.dot(a, b, preferred_element_type=F32)


def silu(z):
    half = 0.5 * z
    return half + half * jnp.tanh(half)


def kernel(
    regions,
    x_hbm, targets_ref, nbr_ref, w_in_hbm, b_ref, gain_ref, wqkv_hbm, wo_hbm, wdec_hbm, whead_hbm,
    out_ref,
    x, w_in, w_in_t, b_t, wqkv, wo, wdec, wdec_t, whead,
    rel, slots, own_slots, code_hi, code_lo, onehot, embed, e2,
    send_n, recv_n, part, ra, ra_l, ra_r, rb, rb_l, rb_r,
    st, qp, bias, acc, top, norm, mixed, md, md_t,
    ssem, rsem, lsem,
):
    r = lax.axis_index("region")
    m = lax.axis_index("mp")
    mps = 4
    up = (lax.rem(r + 1, regions), m)
    down = (lax.rem(r + regions - 1, regions), m)
    right_m = lax.rem(m + 1, mps)
    left_m = lax.rem(m + mps - 1, mps)
    opp_m = lax.rem(m + 2, mps)
    right = (r, right_m)
    left = (r, left_m)
    core = lax.rem(r, 2)
    sibling = (r + 1 - 2 * core, m)

    points = x.shape[1]
    width = embed.shape[0]
    quarter = st.shape[0] // 12
    nodes = 4 * quarter
    half = quarter // 2
    span = 3 * nodes
    neighbours = slots.shape[1]
    heads, head_width = wo.shape[0], wo.shape[1]

    started = []

    def send(name, src, dst, dev):
        i = INDEX[name]
        c = pltpu.make_async_remote_copy(
            src_ref=src, dst_ref=dst, send_sem=ssem.at[i], recv_sem=rsem.at[i],
            device_id=dev, device_id_type=MESH,
        )
        c.start()
        started.append(c)

    def arrived(name, dst, shift=0):
        i = INDEX[name] + shift
        pltpu.make_async_remote_copy(
            src_ref=dst, dst_ref=dst, send_sem=ssem.at[i], recv_sem=rsem.at[i],
            device_id=right, device_id_type=MESH,
        ).wait_recv()

    loads = {}
    for i, (name, src, dst) in enumerate((
        ("w_in", w_in_hbm, w_in), ("x", x_hbm, x), ("wqkv", wqkv_hbm, wqkv.at[m]),
        ("wo", wo_hbm, wo.at[m]), ("wdec", wdec_hbm, wdec), ("whead", whead_hbm, whead),
    )):
        loads[name] = pltpu.make_async_copy(src, dst, lsem.at[i])
        loads[name].start()

    barrier = pltpu.get_barrier_semaphore()
    for dev in (up, down, right, left):
        pl.semaphore_signal(barrier, inc=1, device_id=dev, device_id_type=MESH)

    here = r * nodes
    total = regions * nodes
    t = targets_ref[...] - here
    rel[...] = jnp.where(t < 0, t + total, t)
    b_t[...] = jnp.transpose(jnp.broadcast_to(b_ref[...], (128, width)))
    loads["w_in"].wait()
    w_in_t[...] = jnp.transpose(w_in[...].astype(F32)).astype(BF16)

    pl.semaphore_wait(barrier, 4)

    hq = width // 2
    ho = head_width // 2
    q0, o0 = core * hq, core * ho
    q1, o1 = hq - q0, ho - o0

    def w_part(h, start, size, ref=None):
        rows = pl.ds(pl.multiple_of(start, 16), size)
        return (wqkv.at[h] if ref is None else ref).at[pl.ds(0, 2), rows, :]

    def v_part(h, start, size, ref=None):
        rows = pl.ds(pl.multiple_of(start, 16), size)
        return (wqkv.at[h] if ref is None else ref).at[2, rows, :]

    def o_part(h, start, size, ref=None):
        rows = pl.ds(pl.multiple_of(start, 16), size)
        return (wo.at[h] if ref is None else ref).at[rows, :]

    kinds = {"w": (w_part, q0, q1, hq, wqkv_hbm), "v": (v_part, q0, q1, hq, wqkv_hbm), "o": (o_part, o0, o1, ho, wo_hbm)}

    def weights_first(tag):
        view, mine, _, size, hbm = kinds[tag]
        for name, dev in (("r", right), ("l", left)):
            send(tag + name, view(m, mine, size, hbm), view(m, mine, size), dev)

    def weights_second(tag):
        view, mine, _, size, _ = kinds[tag]
        arrived(tag + "r", view(left_m, mine, size))
        send(tag + "2r", view(left_m, mine, size // 2), view(left_m, mine, size // 2), right)
        send(tag + "s0", view(left_m, mine, size), view(left_m, mine, size), sibling)
        arrived(tag + "l", view(right_m, mine, size))
        late = mine + size // 2
        send(tag + "2l", view(right_m, late, size // 2), view(right_m, late, size // 2), left)
        send(tag + "s1", view(right_m, mine, size), view(right_m, mine, size), sibling)

    def weights_third(tag):
        view, mine, _, size, _ = kinds[tag]
        arrived(tag + "2r", view(opp_m, mine, size // 2))
        send(tag + "s2", view(opp_m, mine, size // 2), view(opp_m, mine, size // 2), sibling)
        late = mine + size // 2
        arrived(tag + "2l", view(opp_m, late, size // 2))
        send(tag + "s3", view(opp_m, late, size // 2), view(opp_m, late, size // 2), sibling)

    def weights_end(tag):
        view, _, other, size, _ = kinds[tag]
        arrived(tag + "s0", view(left_m, other, size))
        arrived(tag + "s1", view(right_m, other, size))
        arrived(tag + "s2", view(opp_m, other, size // 2))
        arrived(tag + "s3", view(opp_m, other + size // 2, size // 2))

    weights_first("w")

    loads["x"].wait()
    z = nn(w_in_t[...], x[...]) + jnp.concatenate([b_t[...]] * (points // 128), axis=1)
    embed[...] = silu(z).astype(BF16)

    def pick(base):
        ids = lax.broadcasted_iota(jnp.int32, (nodes, points), 0) + base
        return (ids == rel[...]).astype(F32).astype(BF16)

    def rows_of(ref, q, start=0, size=quarter, slot=0):
        return ref.at[pl.ds(pl.multiple_of(slot * nodes + q * quarter + start, 16), size)]

    onehot[pl.ds(nodes, nodes), :] = pick(nodes)
    send_n[...] = nt(onehot[pl.ds(nodes, nodes), :], embed[...]).astype(BF16)
    order = (opp_m, right_m, left_m, m)
    for k in range(4):
        send("n%d" % k, rows_of(send_n, order[k]), rows_of(recv_n, order[k]), up)
    weights_first("v")
    weights_first("o")
    onehot[pl.ds(0, nodes), :] = pick(0)
    part[...] = nt(onehot[pl.ds(0, nodes), :], embed[...])

    weights_second("w")

    def both(q, start=0, size=quarter):
        return rows_of(part, q, start, size)[...] + rows_of(recv_n, q, start, size)[...].astype(F32)

    lo, hi = pl.ds(0, half), pl.ds(half, half)
    arrived("n0", rows_of(recv_n, opp_m))
    ra[...] = both(opp_m).astype(BF16)
    send("ar", ra.at[lo], ra_l, right)
    send("al", ra.at[hi], ra_r, left)

    s = jnp.transpose(nbr_ref[...]) - (here - nodes)
    s = jnp.where(s < 0, s + total, s)
    slots[...] = jnp.where(s >= total, s - total, s)
    own_slots[...] = slots[pl.ds(pl.multiple_of(m * quarter, 8), quarter), :]
    groups = quarter // 8
    for i in range(8):
        piece = own_slots[pl.ds(i, groups, stride=8), :]
        cols = slice(i * neighbours, (i + 1) * neighbours)
        code_hi[:, cols] = (piece >> 7) + i * 16
        code_lo[:, cols] = piece & 127
    together = 5 if groups % 5 == 0 else 4

    def count_groups(j, _):
        ids = lax.broadcasted_iota(jnp.int32, (128, 8 * neighbours), 0)
        for u in range(together):
            g = j * together + u
            high = (ids == code_hi[pl.ds(g, 1), :]).astype(F32).astype(BF16)
            low = (ids == code_lo[pl.ds(g, 1), :]).astype(F32).astype(BF16)
            count = nt(high, low)
            log = jnp.where(count > 0.0, jnp.log2(count), ABSENT).reshape(8, 16, 128)
            for c in range(span // 128):
                bias[pl.ds(pl.multiple_of(g * 8, 8), 8), c * 128:(c + 1) * 128] = log[:, c, :]
        return 0

    lax.fori_loop(0, groups // together, count_groups, 0)

    arrived("n1", rows_of(recv_n, right_m))
    rb[0, hi] = both(right_m, half, half).astype(BF16)
    send("br1", rb.at[0, hi], rb_l.at[hi], right)
    arrived("ar", ra_l)
    rb[0, lo] = (both(right_m, 0, half) + ra_l[...].astype(F32)).astype(BF16)
    send("br0", rb.at[0, lo], rb_l.at[lo], right)
    weights_third("w")

    loads["wdec"].wait()
    wdec_t[...] = jnp.transpose(wdec[...].astype(F32)).astype(BF16)
    e2[...] = nn(wdec_t[...], embed[...])

    arrived("n2", rows_of(recv_n, left_m))
    rb[1, lo] = both(left_m, 0, half).astype(BF16)
    send("bl0", rb.at[1, lo], rb_r.at[lo], left)
    arrived("al", ra_r)
    rb[1, hi] = (both(left_m, half, half) + ra_r[...].astype(F32)).astype(BF16)
    send("bl1", rb.at[1, hi], rb_r.at[hi], left)
    weights_second("v")
    weights_second("o")
    loads["wqkv"].wait()
    loads["wo"].wait()
    weights_end("w")
    arrived("n3", rows_of(recv_n, m))
    for name, ref in (("br1", rb_l.at[hi]), ("br0", rb_l.at[lo]), ("bl0", rb_r.at[lo]), ("bl1", rb_r.at[hi])):
        arrived(name, ref)
    mesh_in = both(m) + rb_l[...].astype(F32) + rb_r[...].astype(F32)
    mean = jnp.mean(mesh_in * mesh_in, axis=-1, keepdims=True)
    state = (mesh_in * lax.rsqrt(mean + 1e-05) * gain_ref[...]).astype(BF16)

    def share(ref, slot, tag, out):
        def view(q, start=0, size=quarter):
            return rows_of(ref, q, start, size, slot)

        def pass_on(i, q, start=0, size=quarter):
            for name, to_slot, dev in out:
                send(name + str(i), view(q, start, size), rows_of(ref, q, start, size, to_slot), dev)

        send(tag + "r0", view(m, 0, half), view(m, 0, half), right)
        send(tag + "l1", view(m, half, half), view(m, half, half), left)
        pass_on(0, m)
        send(tag + "r1", view(m, half, half), view(m, half, half), right)
        send(tag + "l0", view(m, 0, half), view(m, 0, half), left)
        yield
        arrived(tag + "r0", view(left_m, 0, half))
        send(tag + "f0", view(left_m, 0, half), view(left_m, 0, half), right)
        pass_on(1, left_m, 0, half)
        arrived(tag + "l1", view(right_m, half, half))
        send(tag + "f1", view(right_m, half, half), view(right_m, half, half), left)
        pass_on(2, right_m, half, half)
        yield
        arrived(tag + "r1", view(left_m, half, half))
        pass_on(3, left_m, half, half)
        arrived(tag + "l0", view(right_m, 0, half))
        pass_on(4, right_m, 0, half)
        yield
        arrived(tag + "f0", view(opp_m, 0, half))
        pass_on(5, opp_m, 0, half)
        arrived(tag + "f1", view(opp_m, half, half))
        pass_on(6, opp_m, half, half)
        yield

    def all_passed(ref, name, slot, shift=0):
        for i in range(7):
            arrived(name + str(i), rows_of(ref, 0, 0, half if i else quarter, slot), shift)

    own = rows_of(st, m, slot=1)
    own[...] = state
    steps = share(st, 1, "s", (("su", 0, up), ("sd", 2, down)))
    next(steps)

    scale = LOG2_E * head_width ** -0.5
    queries = [nn(state, wqkv[h, 0]).astype(BF16) for h in range(heads)]
    for h in range(heads):
        qp[pl.ds(h * quarter, quarter), :] = (nt(queries[h], wqkv[h, 1]) * scale).astype(BF16)
    next(steps)
    weights_third("v")
    weights_third("o")
    next(steps)
    next(steps)

    def attend(slot, first):
        rows = pl.ds(pl.multiple_of(slot * nodes, 128), nodes)
        score = nt(qp[...], st[rows, :])
        here_bias = bias[:, rows]
        raised = []
        scales = []
        for h in range(heads):
            masked = score[h * quarter:(h + 1) * quarter] + here_bias
            new = jnp.max(masked, axis=-1, keepdims=True)
            if not first:
                new = jnp.maximum(new, top[h])
                scales.append(jnp.exp2(top[h] - new))
            power = jnp.exp2(masked - new)
            count = jnp.sum(power, axis=-1, keepdims=True)
            norm[h] = count if first else norm[h] * scales[h] + count
            top[h] = new
            raised.append(power.astype(BF16))
        summed = nn(jnp.concatenate(raised, axis=0), st[rows, :])
        for h in range(heads):
            part_h = summed[h * quarter:(h + 1) * quarter]
            acc[h] = part_h if first else acc[h] * scales[h] + part_h

    attend(1, True)
    all_passed(st, "su", 2 - 2 * core, (INDEX["sd0"] - INDEX["su0"]) * (1 - core))
    attend(2 - 2 * core, False)
    weights_end("v")
    weights_end("o")
    all_passed(st, "su", 2 * core, (INDEX["sd0"] - INDEX["su0"]) * core)
    attend(2 * core, False)

    for h in range(heads):
        out_h = nn((acc[h] / norm[h]).astype(BF16), wqkv[h, 2])
        mixed[:, h * head_width:(h + 1) * head_width] = out_h.astype(BF16)
    attended = nn(mixed[...], wo[...].reshape(heads * head_width, width))
    mesh_out = (own[...].astype(F32) + attended).astype(BF16)
    rows_of(md, m)[...] = nn(mesh_out, wdec[...]).astype(BF16)

    for _ in share(md, 0, "m", (("md", 1, down),)):
        pass

    md_t[...] = jnp.transpose(md[pl.ds(0, nodes), :].astype(F32)).astype(BF16)
    e2[...] += nn(md_t[...], onehot[pl.ds(0, nodes), :])
    loads["whead"].wait()
    all_passed(md, "md", 1)
    md_t[...] = jnp.transpose(md[pl.ds(nodes, nodes), :].astype(F32)).astype(BF16)
    z = e2[...] + nn(md_t[...], onehot[pl.ds(nodes, nodes), :])
    out_ref[...] = nn(whead[...], silu(z).astype(BF16))

    for c in started:
        c.wait_send()


def on_device(grid_state, targets, neighbours, w_in, b_in, mesh_gain, w_qkv, w_out, w_dec, w_head):
    points, channels = grid_state.shape
    nodes, nbr = neighbours.shape
    width = w_in.shape[1]
    quarter = nodes // 4
    half = quarter // 2
    span = 3 * nodes
    heads = 4
    head_width = w_qkv.shape[2]
    out_width = w_head.shape[1]
    regions = lax.axis_size("region")
    vmem = pl.BlockSpec(memory_space=pltpu.VMEM)
    anyw = pl.BlockSpec(memory_space=pl.ANY)
    V = pltpu.VMEM
    out = pl.pallas_call(
        functools.partial(kernel, regions),
        out_shape=jax.ShapeDtypeStruct((out_width, points), F32),
        in_specs=[anyw, vmem, vmem, anyw, vmem, vmem, anyw, anyw, anyw, anyw],
        out_specs=vmem,
        scratch_shapes=[
            V((channels, points), BF16), V((channels, width), BF16), V((width, channels), BF16),
            V((width, 128), F32), V((heads, 3, width, head_width), BF16), V((heads, head_width, width), BF16),
            V((width, width), BF16), V((width, width), BF16), V((out_width, width), BF16),
            V((1, points), jnp.int32), V((nodes, nbr), jnp.int32), V((quarter, nbr), jnp.int32),
            V((quarter // 8, 8 * nbr), jnp.int32), V((quarter // 8, 8 * nbr), jnp.int32),
            V((2 * nodes, points), BF16), V((width, points), BF16), V((width, points), F32),
            V((nodes, width), BF16), V((nodes, width), BF16), V((nodes, width), F32),
            V((quarter, width), BF16), V((half, width), BF16), V((half, width), BF16),
            V((2, quarter, width), BF16), V((quarter, width), BF16), V((quarter, width), BF16),
            V((span, width), BF16), V((heads * quarter, width), BF16), V((quarter, span), F32),
            V((heads, quarter, width), F32), V((heads, quarter, 1), F32), V((heads, quarter, 1), F32),
            V((quarter, heads * head_width), BF16), V((2 * nodes, width), BF16), V((width, nodes), BF16),
            pltpu.SemaphoreType.DMA((len(NAMES),)), pltpu.SemaphoreType.DMA((len(NAMES),)),
            pltpu.SemaphoreType.DMA((6,)),
        ],
        compiler_params=pltpu.CompilerParams(
            collective_id=0, has_side_effects=True, vmem_limit_bytes=56 * 1024 * 1024
        ),
        cost_estimate=pl.CostEstimate(flops=10 * 10 ** 9, bytes_accessed=4 * 10 ** 6, transcendentals=3 * 10 ** 6),
    )(
        grid_state.T, targets.reshape(1, points), neighbours.T, w_in, b_in.reshape(1, width),
        mesh_gain.reshape(1, width), w_qkv, w_out, w_dec, w_head.T,
    )
    return out.T


def solution(mesh):
    placed = (
        P(("region", "mp"), None),
        P(("region", "mp")),
        P("region", None),
        P(),
        P(),
        P(),
        P(None, None, "mp"),
        P("mp", None),
        P(),
        P(),
    )
    return jax.shard_map(
        on_device, mesh=mesh, in_specs=placed, out_specs=P(("region", "mp"), None), check_vma=False
    )
```

time: 71.7 us -> 61.4 us (0.86)
  Pallas kernels: 69 us -> 58.3 us
    pallas_call x1, Pallas kernels: 69 us -> 58.3 us  [on_device(): pl.pallas_call(functools.partial(kernel, regions), out_shape=jax.ShapeDty...]
where the time goes in v2:
time: 61.4 us; the launch traced here: 60.3 us
  Pallas kernels  58.3 us (95%)
  local copies, waits for them, and re-layouts  2.02 us (3%)
    pallas_call x1, Pallas kernels, on_device(): pl.pallas_call(functools.partial(kernel, regions), out_shape=jax.ShapeDty...  58.3 us
    unnamed x1, local copies, waits for them, and re-layouts  2.02 us

profile of v2, /device:TPU:2, one launch (start us, length us, event | category | flops | bytes accessed | tf_op | source)
XLA Modules:
  0.0 60.3 jit_solution(9464398199105238772)
XLA Ops:
  0.0 58.3 %shard_map.100 = f32[84,2048]{1,0:T(8,128)} custom-call(bf16[268,2048]{1,0:T(8,128)(2,1)} %bitcast.8, s32[1,2048]{1,0:T(1,128)} %bitcast.11, s32[32,640]{1,0:T(8,128)} %bitcast.10, bf16[268,512]{1,0:T(8,128)(2,1)} %w_in_hbm.1, f32[1,512]{1,0:T(1,128)} %bitcast.12, f32[1,512]{1,0:T(1,128)} %bitcast.13, bf16[3,512,128]{2,1,0:T(8,128)(2,1)} %wqkv_hbm.1, ...), custom_call_target="tpu_custom_call" | custom-call | flops 10000000000 | bytes 4000000 | tf_op jit(solution)/shard_map/pallas_call | solution.py:372
  58.3 2.0 %copy.12 = f32[2048,84]{0,1:T(8,128)} copy(f32[2048,84]{0,1:T(8,128)} %bitcast.7) | data formatting | bytes 1376256

commit v3 on v2

--- a/solution.py
+++ b/solution.py
@@ -43,9 +43,9 @@
 
 def kernel(
     regions,
-    x_hbm, targets_ref, nbr_ref, w_in_hbm, b_ref, gain_ref, wqkv_hbm, wo_hbm, wdec_hbm, whead_hbm,
+    x_hbm, targets_ref, nbr_hbm, w_in_hbm, b_ref, gain_ref, wqkv_hbm, wo_hbm, wdec_hbm, whead_hbm,
     out_ref,
-    x, w_in, w_in_t, b_t, wqkv, wo, wdec, wdec_t, whead,
+    x, nbr, w_in, w_in_t, b_t, wqkv, wo, wdec, wdec_t, whead,
     rel, slots, own_slots, code_hi, code_lo, onehot, embed, e2,
     send_n, recv_n, part, ra, ra_l, ra_r, rb, rb_l, rb_r,
     st, qp, bias, acc, top, norm, mixed, md, md_t,
@@ -94,7 +94,7 @@
     loads = {}
     for i, (name, src, dst) in enumerate((
         ("w_in", w_in_hbm, w_in), ("x", x_hbm, x), ("wqkv", wqkv_hbm, wqkv.at[m]),
-        ("wo", wo_hbm, wo.at[m]), ("wdec", wdec_hbm, wdec), ("whead", whead_hbm, whead),
+        ("wo", wo_hbm, wo.at[m]), ("wdec", wdec_hbm, wdec), ("whead", whead_hbm, whead), ("nbr", nbr_hbm, nbr),
     )):
         loads[name] = pltpu.make_async_copy(src, dst, lsem.at[i])
         loads[name].start()
@@ -108,9 +108,6 @@
     t = targets_ref[...] - here
     rel[...] = jnp.where(t < 0, t + total, t)
     b_t[...] = jnp.transpose(jnp.broadcast_to(b_ref[...], (128, width)))
-    loads["w_in"].wait()
-    w_in_t[...] = jnp.transpose(w_in[...].astype(F32)).astype(BF16)
-
     pl.semaphore_wait(barrier, 4)
 
     hq = width // 2
@@ -162,41 +159,47 @@
         arrived(tag + "s2", view(opp_m, other, size // 2))
         arrived(tag + "s3", view(opp_m, other + size // 2, size // 2))
 
-    weights_first("w")
-
+    for tag in ("w", "v", "o"):
+        weights_first(tag)
+
+    loads["w_in"].wait()
+    w_in_t[...] = jnp.transpose(w_in[...].astype(F32)).astype(BF16)
     loads["x"].wait()
     z = nn(w_in_t[...], x[...]) + jnp.concatenate([b_t[...]] * (points // 128), axis=1)
     embed[...] = silu(z).astype(BF16)
 
-    def pick(base):
-        ids = lax.broadcasted_iota(jnp.int32, (nodes, points), 0) + base
-        return (ids == rel[...]).astype(F32).astype(BF16)
+    order = (opp_m, right_m, left_m, m)
 
     def rows_of(ref, q, start=0, size=quarter, slot=0):
-        return ref.at[pl.ds(pl.multiple_of(slot * nodes + q * quarter + start, 16), size)]
-
-    onehot[pl.ds(nodes, nodes), :] = pick(nodes)
-    send_n[...] = nt(onehot[pl.ds(nodes, nodes), :], embed[...]).astype(BF16)
-    order = (opp_m, right_m, left_m, m)
-    for k in range(4):
-        send("n%d" % k, rows_of(send_n, order[k]), rows_of(recv_n, order[k]), up)
-    weights_first("v")
-    weights_first("o")
-    onehot[pl.ds(0, nodes), :] = pick(0)
-    part[...] = nt(onehot[pl.ds(0, nodes), :], embed[...])
-
-    weights_second("w")
+        first = slot * nodes + q * quarter + start
+        return ref.at[pl.ds(first if isinstance(first, int) else pl.multiple_of(first, 16), size)]
+
+    def sums(slot, k, count):
+        for i in range(k, k + count):
+            ids = lax.broadcasted_iota(jnp.int32, (quarter, points), 0) + (slot * nodes + order[i] * quarter)
+            rows_of(onehot, i, slot=slot)[...] = (ids == rel[...]).astype(F32).astype(BF16)
+        return nt(rows_of(onehot, k, 0, count * quarter, slot)[...], embed[...])
+
+    for k in (0, 2):
+        rows_of(send_n, k, 0, 2 * quarter)[...] = sums(1, k, 2).astype(BF16)
+        for i in (k, k + 1):
+            send("n%d" % i, rows_of(send_n, i), rows_of(recv_n, i), up)
+    part[...] = sums(0, 0, 4)
+
+    for tag in ("w", "v", "o"):
+        weights_second(tag)
 
     def both(q, start=0, size=quarter):
         return rows_of(part, q, start, size)[...] + rows_of(recv_n, q, start, size)[...].astype(F32)
 
     lo, hi = pl.ds(0, half), pl.ds(half, half)
-    arrived("n0", rows_of(recv_n, opp_m))
-    ra[...] = both(opp_m).astype(BF16)
+    arrived("n0", rows_of(recv_n, 0))
+    ra[...] = both(0).astype(BF16)
     send("ar", ra.at[lo], ra_l, right)
     send("al", ra.at[hi], ra_r, left)
 
-    s = jnp.transpose(nbr_ref[...]) - (here - nodes)
+    loads["nbr"].wait()
+    s = jnp.transpose(nbr[...]) - (here - nodes)
     s = jnp.where(s < 0, s + total, s)
     slots[...] = jnp.where(s >= total, s - total, s)
     own_slots[...] = slots[pl.ds(pl.multiple_of(m * quarter, 8), quarter), :]
@@ -222,11 +225,11 @@
 
     lax.fori_loop(0, groups // together, count_groups, 0)
 
-    arrived("n1", rows_of(recv_n, right_m))
-    rb[0, hi] = both(right_m, half, half).astype(BF16)
+    arrived("n1", rows_of(recv_n, 1))
+    rb[0, hi] = both(1, half, half).astype(BF16)
     send("br1", rb.at[0, hi], rb_l.at[hi], right)
     arrived("ar", ra_l)
-    rb[0, lo] = (both(right_m, 0, half) + ra_l[...].astype(F32)).astype(BF16)
+    rb[0, lo] = (both(1, 0, half) + ra_l[...].astype(F32)).astype(BF16)
     send("br0", rb.at[0, lo], rb_l.at[lo], right)
     weights_third("w")
 
@@ -234,63 +237,68 @@
     wdec_t[...] = jnp.transpose(wdec[...].astype(F32)).astype(BF16)
     e2[...] = nn(wdec_t[...], embed[...])
 
-    arrived("n2", rows_of(recv_n, left_m))
-    rb[1, lo] = both(left_m, 0, half).astype(BF16)
+    arrived("n2", rows_of(recv_n, 2))
+    rb[1, lo] = both(2, 0, half).astype(BF16)
     send("bl0", rb.at[1, lo], rb_r.at[lo], left)
     arrived("al", ra_r)
-    rb[1, hi] = (both(left_m, half, half) + ra_r[...].astype(F32)).astype(BF16)
+    rb[1, hi] = (both(2, half, half) + ra_r[...].astype(F32)).astype(BF16)
     send("bl1", rb.at[1, hi], rb_r.at[hi], left)
-    weights_second("v")
-    weights_second("o")
     loads["wqkv"].wait()
     loads["wo"].wait()
     weights_end("w")
-    arrived("n3", rows_of(recv_n, m))
+    arrived("n3", rows_of(recv_n, 3))
     for name, ref in (("br1", rb_l.at[hi]), ("br0", rb_l.at[lo]), ("bl0", rb_r.at[lo]), ("bl1", rb_r.at[hi])):
         arrived(name, ref)
-    mesh_in = both(m) + rb_l[...].astype(F32) + rb_r[...].astype(F32)
+    mesh_in = both(3) + rb_l[...].astype(F32) + rb_r[...].astype(F32)
     mean = jnp.mean(mesh_in * mesh_in, axis=-1, keepdims=True)
     state = (mesh_in * lax.rsqrt(mean + 1e-05) * gain_ref[...]).astype(BF16)
 
-    def share(ref, slot, tag, out):
-        def view(q, start=0, size=quarter):
-            return rows_of(ref, q, start, size, slot)
-
-        def pass_on(i, q, start=0, size=quarter):
+    def share(ref, slot, tag, out, here_at, there_at):
+        def view(at, who, start=0, size=quarter, to_slot=slot):
+            return rows_of(ref, at[who], start, size, to_slot)
+
+        def give(name, who, whose, start, dev):
+            send(tag + name, view(here_at, who, start, half), view(there_at(who, whose), whose, start, half), dev)
+
+        def got(name, who, start):
+            arrived(tag + name, view(here_at, who, start, half))
+
+        def pass_on(i, who, start=0, size=quarter):
             for name, to_slot, dev in out:
-                send(name + str(i), view(q, start, size), rows_of(ref, q, start, size, to_slot), dev)
-
-        send(tag + "r0", view(m, 0, half), view(m, 0, half), right)
-        send(tag + "l1", view(m, half, half), view(m, half, half), left)
-        pass_on(0, m)
-        send(tag + "r1", view(m, half, half), view(m, half, half), right)
-        send(tag + "l0", view(m, 0, half), view(m, 0, half), left)
+                send(name + str(i), view(here_at, who, start, size), view(here_at, who, start, size, to_slot), dev)
+
+        give("r0", "own", "left", 0, right)
+        give("l1", "own", "right", half, left)
+        pass_on(0, "own")
+        give("r1", "own", "left", half, right)
+        give("l0", "own", "right", 0, left)
         yield
-        arrived(tag + "r0", view(left_m, 0, half))
-        send(tag + "f0", view(left_m, 0, half), view(left_m, 0, half), right)
-        pass_on(1, left_m, 0, half)
-        arrived(tag + "l1", view(right_m, half, half))
-        send(tag + "f1", view(right_m, half, half), view(right_m, half, half), left)
-        pass_on(2, right_m, half, half)
+        got("r0", "left", 0)
+        give("f0", "left", "opp", 0, right)
+        pass_on(1, "left", 0, half)
+        got("l1", "right", half)
+        give("f1", "right", "opp", half, left)
+        pass_on(2, "right", half, half)
         yield
-        arrived(tag + "r1", view(left_m, half, half))
-        pass_on(3, left_m, half, half)
-        arrived(tag + "l0", view(right_m, 0, half))
-        pass_on(4, right_m, 0, half)
+        got("r1", "left", half)
+        pass_on(3, "left", half, half)
+        got("l0", "right", 0)
+        pass_on(4, "right", 0, half)
         yield
-        arrived(tag + "f0", view(opp_m, 0, half))
-        pass_on(5, opp_m, 0, half)
-        arrived(tag + "f1", view(opp_m, half, half))
-        pass_on(6, opp_m, half, half)
+        got("f0", "opp", 0)
+        pass_on(5, "opp", 0, half)
+        got("f1", "opp", half)
+        pass_on(6, "opp", half, half)
         yield
 
-    def all_passed(ref, name, slot, shift=0):
-        for i in range(7):
+    def all_passed(ref, name, slot, shift=0, which=range(7)):
+        for i in which:
             arrived(name + str(i), rows_of(ref, 0, 0, half if i else quarter, slot), shift)
 
     own = rows_of(st, m, slot=1)
     own[...] = state
-    steps = share(st, 1, "s", (("su", 0, up), ("sd", 2, down)))
+    by_number = {"own": m, "left": left_m, "right": right_m, "opp": opp_m}
+    steps = share(st, 1, "s", (("su", 0, up), ("sd", 2, down)), by_number, lambda who, whose: {whose: by_number[who]})
     next(steps)
 
     scale = LOG2_E * head_width ** -0.5
@@ -338,18 +346,28 @@
         mixed[:, h * head_width:(h + 1) * head_width] = out_h.astype(BF16)
     attended = nn(mixed[...], wo[...].reshape(heads * head_width, width))
     mesh_out = (own[...].astype(F32) + attended).astype(BF16)
-    rows_of(md, m)[...] = nn(mesh_out, wdec[...]).astype(BF16)
-
-    for _ in share(md, 0, "m", (("md", 1, down),)):
+    rows_of(md, 3)[...] = nn(mesh_out, wdec[...]).astype(BF16)
+
+    by_place = {"own": 3, "left": 2, "right": 1, "opp": 0}
+    for _ in share(md, 0, "m", (("md", 1, down),), by_place, lambda who, whose: by_place):
         pass
 
-    md_t[...] = jnp.transpose(md[pl.ds(0, nodes), :].astype(F32)).astype(BF16)
-    e2[...] += nn(md_t[...], onehot[pl.ds(0, nodes), :])
+    def turned(first, count):
+        return jnp.transpose(md[pl.ds(first, count), :].astype(F32)).astype(BF16)
+
+    e2[...] += nn(turned(0, nodes), onehot[pl.ds(0, nodes), :])
     loads["whead"].wait()
-    all_passed(md, "md", 1)
-    md_t[...] = jnp.transpose(md[pl.ds(nodes, nodes), :].astype(F32)).astype(BF16)
-    z = e2[...] + nn(md_t[...], onehot[pl.ds(nodes, nodes), :])
-    out_ref[...] = nn(whead[...], silu(z).astype(BF16))
+    all_passed(md, "md", 1, which=range(5))
+    late = -(-quarter // 128) * 128
+    if late < nodes:
+        e2[...] += nn(turned(nodes + late, nodes - late), onehot[pl.ds(nodes + late, nodes - late), :])
+    all_passed(md, "md", 1, which=(5, 6))
+    md_t[...] = turned(nodes, late)
+    block = min(1024, points)
+    for i in range(points // block):
+        cols = slice(i * block, (i + 1) * block)
+        z = e2[:, cols] + nn(md_t[...], onehot[nodes:nodes + late, cols])
+        out_ref[:, cols] = nn(whead[...], silu(z).astype(BF16))
 
     for c in started:
         c.wait_send()
@@ -371,11 +389,11 @@
     V = pltpu.VMEM
     out = pl.pallas_call(
         functools.partial(kernel, regions),
-        out_shape=jax.ShapeDtypeStruct((out_width, points), F32),
-        in_specs=[anyw, vmem, vmem, anyw, vmem, vmem, anyw, anyw, anyw, anyw],
+        out_shape=pltpu.VMEM((out_width, points), F32),
+        in_specs=[anyw, vmem, anyw, anyw, vmem, vmem, anyw, anyw, anyw, anyw],
         out_specs=vmem,
         scratch_shapes=[
-            V((channels, points), BF16), V((channels, width), BF16), V((width, channels), BF16),
+            V((channels, points), BF16), V((nbr, nodes), jnp.int32), V((channels, width), BF16), V((width, channels), BF16),
             V((width, 128), F32), V((heads, 3, width, head_width), BF16), V((heads, head_width, width), BF16),
             V((width, width), BF16), V((width, width), BF16), V((out_width, width), BF16),
             V((1, points), jnp.int32), V((nodes, nbr), jnp.int32), V((quarter, nbr), jnp.int32),
@@ -386,9 +404,9 @@
             V((2, quarter, width), BF16), V((quarter, width), BF16), V((quarter, width), BF16),
             V((span, width), BF16), V((heads * quarter, width), BF16), V((quarter, span), F32),
             V((heads, quarter, width), F32), V((heads, quarter, 1), F32), V((heads, quarter, 1), F32),
-            V((quarter, heads * head_width), BF16), V((2 * nodes, width), BF16), V((width, nodes), BF16),
+            V((quarter, heads * head_width), BF16), V((2 * nodes, width), BF16), V((width, -(-quarter // 128) * 128), BF16),
             pltpu.SemaphoreType.DMA((len(NAMES),)), pltpu.SemaphoreType.DMA((len(NAMES),)),
-            pltpu.SemaphoreType.DMA((6,)),
+            pltpu.SemaphoreType.DMA((7,)),
         ],
         compiler_params=pltpu.CompilerParams(
             collective_id=0, has_side_effects=True, vmem_limit_bytes=56 * 1024 * 1024

time: 61.4 us -> 59 us (0.961); the launches traced: 60.3 us -> 58.8 us
  local copies, waits for them, and re-layouts: 2.02 us -> 0.86 us
    unnamed x1, local copies, waits for them, and re-layouts: 2.02 us -> 0.86 us
where the time goes in v3:
time: 59 us; the launch traced here: 58.8 us
  Pallas kernels  57.9 us (98%)
  local copies, waits for them, and re-layouts  0.86 us (1%)
    pallas_call x1, Pallas kernels, on_device(): pl.pallas_call(functools.partial(kernel, regions), out_shape=pltpu.VMEM((...  57.9 us

profile of v3, /device:TPU:2, one launch (start us, length us, event | category | flops | bytes accessed | tf_op | source)
XLA Modules:
  0.0 58.8 jit_solution(14136451738689876358)
XLA Ops:
  0.0 57.9 %shard_map.100 = f32[84,2048]{1,0:T(8,128)S(1)} custom-call(bf16[268,2048]{1,0:T(8,128)(2,1)} %bitcast.8, s32[1,2048]{1,0:T(1,128)} %bitcast.11, s32[32,640]{1,0:T(8,128)} %bitcast.10, bf16[268,512]{1,0:T(8,128)(2,1)} %w_in_hbm.1, f32[1,512]{1,0:T(1,128)} %bitcast.12, f32[1,512]{1,0:T(1,128)} %bitcast.13, bf16[3,512,128]{2,1,0:T(8,128)(2,1)} %wqkv_hbm.1, ...), custom_call_target="tpu_custom_call" | custom-call | flops 10000000000 | bytes 4000000 | tf_op jit(solution)/shard_map/pallas_call | solution.py:390
  57.9 0.9 %copy.12 = f32[2048,84]{0,1:T(8,128)} copy(f32[2048,84]{0,1:T(8,128)S(1)} %bitcast.7) | data formatting | bytes 1376256

commit v4 on v3

v4 whole, which is shorter than its diff:
```python
import functools

import jax
import jax.numpy as jnp
from jax import lax
from jax.experimental import pallas as pl
from jax.experimental.pallas import tpu as pltpu
from jax.sharding import PartitionSpec as P

MESH = pl.DeviceIdType.MESH
BF16 = jnp.bfloat16
F32 = jnp.float32
LOG2_E = 1.4426950408889634
ABSENT = -1e30

NAMES = (
    *("or", "ol", "oo", "os0", "os1", "os2"),
    *("n0", "n1", "n2", "n3"),
    *("ar", "al", "br0", "br1", "bl0", "bl1"),
    *("sr0", "sr1", "sl0", "sl1", "sf0", "sf1"),
    *("su0", "su1", "su2", "su3", "su4", "su5", "su6"),
    *("sd0", "sd1", "sd2", "sd3", "sd4", "sd5", "sd6"),
    *("xr", "xl", "xo"),
    *("mr0", "mr1", "ml0", "ml1", "mf0", "mf1"),
    *("md0", "md1", "md2", "md3", "md4", "md5", "md6"),
)
INDEX = {name: i for i, name in enumerate(NAMES)}


def nt(a, b):
    return lax.dot_general(a, b, (((1,), (1,)), ((), ())), preferred_element_type=F32)


def nn(a, b):
    return jnp.dot(a, b, preferred_element_type=F32)


def silu(z):
    half = 0.5 * z
    return half + half * jnp.tanh(half)


def kernel(
    regions,
    x_hbm, targets_ref, nbr_hbm, w_in_hbm, b_ref, gain_ref, wqkv_hbm, wo_hbm, wdec_hbm, whead_hbm,
    out_ref,
    x, nbr, w_in, w_in_t, b_t, wqkv, wo, wdec, wdec_t, whead,
    rel, slots, code_hi, code_lo, onehot, embed, e2,
    send_n, recv_n, part, ra, ra_l, ra_r, rb, rb_l, rb_r,
    st, query, kv, bias, acc, top, norm, mixed, mix_out, md, md_t,
    ssem, rsem, lsem,
):
    r = lax.axis_index("region")
    m = lax.axis_index("mp")
    mps = 4
    up = (lax.rem(r + 1, regions), m)
    down = (lax.rem(r + regions - 1, regions), m)
    right_m = lax.rem(m + 1, mps)
    left_m = lax.rem(m + mps - 1, mps)
    opp_m = lax.rem(m + 2, mps)
    opposite = (r, opp_m)
    right = (r, right_m)
    left = (r, left_m)
    core = lax.rem(r, 2)
    sibling = (r + 1 - 2 * core, m)

    points = x.shape[1]
    width = embed.shape[0]
    nodes = st.shape[0]
    quarter = nodes // 4
    half = quarter // 2
    span = 3 * nodes
    neighbours = slots.shape[1]
    heads, head_width = wo.shape[0], wo.shape[1]

    started = []

    def send(name, src, dst, dev):
        i = INDEX[name]
        c = pltpu.make_async_remote_copy(
            src_ref=src, dst_ref=dst, send_sem=ssem.at[i], recv_sem=rsem.at[i],
            device_id=dev, device_id_type=MESH,
        )
        c.start()
        started.append(c)

    def arrived(name, dst, shift=0):
        i = INDEX[name] + shift
        pltpu.make_async_remote_copy(
            src_ref=dst, dst_ref=dst, send_sem=ssem.at[i], recv_sem=rsem.at[i],
            device_id=right, device_id_type=MESH,
        ).wait_recv()

    loads = {}
    for i, (name, src, dst) in enumerate((
        ("w_in", w_in_hbm, w_in), ("x", x_hbm, x), ("wo", wo_hbm, wo.at[m]), ("wdec", wdec_hbm, wdec), ("whead", whead_hbm, whead), ("nbr", nbr_hbm, nbr),
        *(("w%d" % j, wqkv_hbm.at[j], wqkv.at[:, pl.ds(j * head_width, head_width)]) for j in range(3)),
    )):
        loads[name] = pltpu.make_async_copy(src, dst, lsem.at[i])
        loads[name].start()

    barrier = pltpu.get_barrier_semaphore()
    for dev in (up, down, right, left, opposite):
        pl.semaphore_signal(barrier, inc=1, device_id=dev, device_id_type=MESH)

    here = r * nodes
    total = regions * nodes
    t = targets_ref[...] - here
    rel[...] = jnp.where(t < 0, t + total, t)
    b_t[...] = jnp.transpose(jnp.broadcast_to(b_ref[...], (128, width)))
    pl.semaphore_wait(barrier, 5)

    ho = head_width // 2

    def wo_half(h, which):
        return wo.at[h, pl.ds(pl.multiple_of(which * ho, 16), ho), :]

    for name, dev in (("or", right), ("ol", left), ("oo", opposite)):
        send(name, wo_hbm.at[pl.ds(pl.multiple_of(core * ho, 16), ho), :], wo_half(m, core), dev)

    loads["w_in"].wait()
    w_in_t[...] = jnp.transpose(w_in[...].astype(F32)).astype(BF16)
    loads["x"].wait()
    z = nn(w_in_t[...], x[...]) + jnp.concatenate([b_t[...]] * (points // 128), axis=1)
    embed[...] = silu(z).astype(BF16)

    order = (opp_m, right_m, left_m, m)

    def rows_of(ref, q, start=0, size=quarter, slot=0):
        first = slot * nodes + q * quarter + start
        return ref.at[pl.ds(first if isinstance(first, int) else pl.multiple_of(first, 16), size)]

    def sums(slot, k, count):
        for i in range(k, k + count):
            ids = lax.broadcasted_iota(jnp.int32, (quarter, points), 0) + (slot * nodes + order[i] * quarter)
            rows_of(onehot, i, slot=slot)[...] = (ids == rel[...]).astype(F32).astype(BF16)
        return nt(rows_of(onehot, k, 0, count * quarter, slot)[...], embed[...])

    for k in (0, 2):
        rows_of(send_n, k, 0, 2 * quarter)[...] = sums(1, k, 2).astype(BF16)
        for i in (k, k + 1):
            send("n%d" % i, rows_of(send_n, i), rows_of(recv_n, i), up)
    part[...] = sums(0, 0, 4)

    for i, (name, h) in enumerate((("or", left_m), ("ol", right_m), ("oo", opp_m))):
        arrived(name, wo_half(h, core))
        send("os%d" % i, wo_half(h, core), wo_half(h, core), sibling)

    def both(q, start=0, size=quarter):
        return rows_of(part, q, start, size)[...] + rows_of(recv_n, q, start, size)[...].astype(F32)

    lo, hi = pl.ds(0, half), pl.ds(half, half)
    arrived("n0", rows_of(recv_n, 0))
    ra[...] = both(0).astype(BF16)
    send("ar", ra.at[lo], ra_l, right)
    send("al", ra.at[hi], ra_r, left)

    loads["nbr"].wait()
    s = jnp.transpose(nbr[...]) - (here - nodes)
    s = jnp.where(s < 0, s + total, s)
    slots[...] = jnp.where(s >= total, s - total, s)
    groups = nodes // 8
    for i in range(8):
        piece = slots[pl.ds(i, groups, stride=8), :]
        cols = slice(i * neighbours, (i + 1) * neighbours)
        code_hi[:, cols] = (piece >> 7) + i * 16
        code_lo[:, cols] = piece & 127
    together = 5 if groups % 20 == 0 else 4
    share_of_counts = groups // (4 * together)

    def count_groups(j, _):
        ids = lax.broadcasted_iota(jnp.int32, (128, 8 * neighbours), 0)
        for u in range(together):
            g = j * together + u
            high = (ids == code_hi[pl.ds(g, 1), :]).astype(F32).astype(BF16)
            low = (ids == code_lo[pl.ds(g, 1), :]).astype(F32).astype(BF16)
            count = nt(high, low)
            log = jnp.where(count > 0.0, jnp.log2(count), ABSENT).reshape(8, 16, 128)
            for c in range(span // 128):
                bias[pl.ds(pl.multiple_of(g * 8, 8), 8), c * 128:(c + 1) * 128] = log[:, c, :]
        return 0

    def counts(i):
        lax.fori_loop(i * share_of_counts, (i + 1) * share_of_counts, count_groups, 0)

    counts(0)
    counts(1)

    arrived("n1", rows_of(recv_n, 1))
    rb[0, hi] = both(1, half, half).astype(BF16)
    send("br1", rb.at[0, hi], rb_l.at[hi], right)
    arrived("ar", ra_l)
    rb[0, lo] = (both(1, 0, half) + ra_l[...].astype(F32)).astype(BF16)
    send("br0", rb.at[0, lo], rb_l.at[lo], right)
    arrived("n2", rows_of(recv_n, 2))
    rb[1, lo] = both(2, 0, half).astype(BF16)
    send("bl0", rb.at[1, lo], rb_r.at[lo], left)
    arrived("al", ra_r)
    rb[1, hi] = (both(2, half, half) + ra_r[...].astype(F32)).astype(BF16)
    send("bl1", rb.at[1, hi], rb_r.at[hi], left)
    arrived("n3", rows_of(recv_n, 3))
    for name, ref in (("br1", rb_l.at[hi]), ("br0", rb_l.at[lo]), ("bl0", rb_r.at[lo]), ("bl1", rb_r.at[hi])):
        arrived(name, ref)
    mesh_in = both(3) + rb_l[...].astype(F32) + rb_r[...].astype(F32)
    mean = jnp.mean(mesh_in * mesh_in, axis=-1, keepdims=True)
    state = (mesh_in * lax.rsqrt(mean + 1e-05) * gain_ref[...]).astype(BF16)

    def share(ref, tag, here_at, there_at, pass_on):
        def view(at, who, start=0, size=quarter):
            return rows_of(ref, at[who], start, size)

        def give(name, who, whose, start, dev):
            send(tag + name, view(here_at, who, start, half), view(there_at(who, whose), whose, start, half), dev)

        def got(name, who, start):
            arrived(tag + name, view(here_at, who, start, half))

        give("r0", "own", "left", 0, right)
        give("l1", "own", "right", half, left)
        pass_on(0, "own", 0, quarter)
        give("r1", "own", "left", half, right)
        give("l0", "own", "right", 0, left)
        yield
        got("r0", "left", 0)
        give("f0", "left", "opp", 0, right)
        pass_on(1, "left", 0, half)
        got("l1", "right", half)
        give("f1", "right", "opp", half, left)
        pass_on(2, "right", half, half)
        yield
        got("r1", "left", half)
        pass_on(3, "left", half, half)
        got("l0", "right", 0)
        pass_on(4, "right", 0, half)
        yield
        got("f0", "opp", 0)
        pass_on(5, "opp", 0, half)
        got("f1", "opp", half)
        pass_on(6, "opp", half, half)
        yield

    def all_passed(ref, name, slot, shift=0, which=range(7)):
        for i in which:
            arrived(name + str(i), rows_of(ref, 0, 0, half if i else quarter, slot), shift)

    own = rows_of(st, m)
    own[...] = state
    by_number = {"own": m, "left": left_m, "right": right_m, "opp": opp_m}
    pieces = []
    steps = share(st, "s", by_number, lambda who, whose: {whose: by_number[who]}, lambda *piece: pieces.append(piece))

    def project():
        new = jnp.concatenate([rows_of(st, by_number[who], start, size)[...] for _, who, start, size in pieces], axis=0)
        qkv = nn(new, wqkv[...])
        first = 0
        for i, who, start, size in pieces:
            rows = qkv[first:first + size]
            first += size
            rows_of(query, by_number[who], start, size)[...] = (rows[:, :head_width] * scale).astype(BF16)
            rows_of(kv, by_number[who], start, size, 1)[...] = rows[:, head_width:].astype(BF16)
            for name, slot, dev in (("su", 0, up), ("sd", 2, down)):
                send(name + str(i), rows_of(kv, by_number[who], start, size, 1), rows_of(kv, by_number[who], start, size, slot), dev)
        pieces.clear()

    scale = LOG2_E * head_width ** -0.5
    next(steps)
    for j in range(3):
        loads["w%d" % j].wait()
    project()
    counts(2)
    next(steps)
    project()
    counts(3)
    next(steps)
    project()

    loads["wdec"].wait()
    wdec_t[...] = jnp.transpose(wdec[...].astype(F32)).astype(BF16)
    e2[...] = nn(wdec_t[...], embed[...])
    next(steps)
    project()

    def attend(slot, first):
        rows = pl.ds(pl.multiple_of(slot * nodes, 128), nodes)
        masked = nt(query[...], kv[rows, :head_width]) + bias[:, rows]
        new = jnp.max(masked, axis=-1, keepdims=True)
        if not first:
            new = jnp.maximum(new, top[...])
            old = jnp.exp2(top[...] - new)
        power = jnp.exp2(masked - new)
        count = jnp.sum(power, axis=-1, keepdims=True)
        summed = nn(power.astype(BF16), kv[rows, head_width:])
        norm[...] = count if first else norm[...] * old + count
        acc[...] = summed if first else acc[...] * old + summed
        top[...] = new

    shift = INDEX["sd0"] - INDEX["su0"]
    attend(1, True)
    all_passed(kv, "su", 2 - 2 * core, shift * (1 - core))
    attend(2 - 2 * core, False)
    all_passed(kv, "su", 2 * core, shift * core)
    attend(2 * core, False)

    mix_out[...] = (acc[...] / norm[...]).astype(BF16)
    mine = pl.ds(pl.multiple_of(m * head_width, 128), head_width)
    for name, q, dev in (("xr", right_m, right), ("xl", left_m, left), ("xo", opp_m, opposite)):
        send(name, rows_of(mix_out, q), mixed.at[:, mine], dev)
    mixed[:, mine] = rows_of(mix_out, m)[...]
    loads["wo"].wait()
    for i, h in enumerate((left_m, right_m, opp_m)):
        arrived("os%d" % i, wo_half(h, 1 - core))
    for name in ("xr", "xl", "xo"):
        arrived(name, mixed.at[:, mine])
    attended = nn(mixed[...], wo[...].reshape(heads * head_width, width))
    mesh_out = (own[...].astype(F32) + attended).astype(BF16)
    rows_of(md, 3)[...] = nn(mesh_out, wdec[...]).astype(BF16)

    by_place = {"own": 3, "left": 2, "right": 1, "opp": 0}

    def to_the_region_before(i, who, start, size):
        at = by_place[who]
        send("md%d" % i, rows_of(md, at, start, size), rows_of(md, at, start, size, 1), down)

    for _ in share(md, "m", by_place, lambda who, whose: by_place, to_the_region_before):
        pass

    def turned(first, count):
        return jnp.transpose(md[pl.ds(first, count), :].astype(F32)).astype(BF16)

    e2[...] += nn(turned(0, nodes), onehot[pl.ds(0, nodes), :])
    loads["whead"].wait()
    all_passed(md, "md", 1, which=range(5))
    late = -(-quarter // 128) * 128
    if late < nodes:
        e2[...] += nn(turned(nodes + late, nodes - late), onehot[pl.ds(nodes + late, nodes - late), :])
    all_passed(md, "md", 1, which=(5, 6))
    md_t[...] = turned(nodes, late)
    block = min(1024, points)
    for i in range(points // block):
        cols = slice(i * block, (i + 1) * block)
        z = e2[:, cols] + nn(md_t[...], onehot[nodes:nodes + late, cols])
        out_ref[:, cols] = nn(whead[...], silu(z).astype(BF16))

    for c in started:
        c.wait_send()


def on_device(grid_state, targets, neighbours, w_in, b_in, mesh_gain, w_qkv, w_out, w_dec, w_head):
    points, channels = grid_state.shape
    nodes, nbr = neighbours.shape
    width = w_in.shape[1]
    quarter = nodes // 4
    half = quarter // 2
    span = 3 * nodes
    heads = 4
    head_width = w_qkv.shape[2]
    out_width = w_head.shape[1]
    regions = lax.axis_size("region")
    vmem = pl.BlockSpec(memory_space=pltpu.VMEM)
    anyw = pl.BlockSpec(memory_space=pl.ANY)
    V = pltpu.VMEM
    out = pl.pallas_call(
        functools.partial(kernel, regions),
        out_shape=pltpu.VMEM((out_width, points), F32),
        in_specs=[anyw, vmem, anyw, anyw, vmem, vmem, anyw, anyw, anyw, anyw],
        out_specs=vmem,
        scratch_shapes=[
            V((channels, points), BF16), V((nbr, nodes), jnp.int32), V((channels, width), BF16),
            V((width, channels), BF16), V((width, 128), F32), V((width, 3 * head_width), BF16),
            V((heads, head_width, width), BF16), V((width, width), BF16), V((width, width), BF16),
            V((out_width, width), BF16),
            V((1, points), jnp.int32), V((nodes, nbr), jnp.int32),
            V((nodes // 8, 8 * nbr), jnp.int32), V((nodes // 8, 8 * nbr), jnp.int32),
            V((2 * nodes, points), BF16), V((width, points), BF16), V((width, points), F32),
            V((nodes, width), BF16), V((nodes, width), BF16), V((nodes, width), F32),
            V((quarter, width), BF16), V((half, width), BF16), V((half, width), BF16),
            V((2, quarter, width), BF16), V((quarter, width), BF16), V((quarter, width), BF16),
            V((nodes, width), BF16), V((nodes, head_width), BF16), V((span, 2 * head_width), BF16),
            V((nodes, span), F32), V((nodes, head_width), F32), V((nodes, 1), F32), V((nodes, 1), F32),
            V((quarter, heads * head_width), BF16), V((nodes, head_width), BF16),
            V((2 * nodes, width), BF16), V((width, -(-quarter // 128) * 128), BF16),
            pltpu.SemaphoreType.DMA((len(NAMES),)), pltpu.SemaphoreType.DMA((len(NAMES),)),
            pltpu.SemaphoreType.DMA((9,)),
        ],
        compiler_params=pltpu.CompilerParams(
            collective_id=0, has_side_effects=True, vmem_limit_bytes=56 * 1024 * 1024
        ),
        cost_estimate=pl.CostEstimate(flops=10 * 10 ** 9, bytes_accessed=4 * 10 ** 6, transcendentals=3 * 10 ** 6),
    )(
        grid_state.T, targets.reshape(1, points), neighbours.T, w_in, b_in.reshape(1, width),
        mesh_gain.reshape(1, width), w_qkv, w_out, w_dec, w_head.T,
    )
    return out.T


def solution(mesh):
    placed = (
        P(("region", "mp"), None),
        P(("region", "mp")),
        P("region", None),
        P(),
        P(),
        P(),
        P(None, None, "mp"),
        P("mp", None),
        P(),
        P(),
    )
    return jax.shard_map(
        on_device, mesh=mesh, in_specs=placed, out_specs=P(("region", "mp"), None), check_vma=False
    )
```

time: 59 us -> 60 us (1.017)
  Pallas kernels: 57.9 us -> 59 us
    pallas_call x1, Pallas kernels: 57.9 us -> 59 us  [on_device(): pl.pallas_call(functools.partial(kernel, regions), out_shape=pltpu.VMEM((...]
where the time goes in v4:
time: 60 us; the launch traced here: 59.8 us
  Pallas kernels  59 us (98%)
  local copies, waits for them, and re-layouts  0.86 us (1%)
    pallas_call x1, Pallas kernels, on_device(): pl.pallas_call(functools.partial(kernel, regions), out_shape=pltpu.VMEM((...  59 us

profile of v4, /device:TPU:2, one launch (start us, length us, event | category | flops | bytes accessed | tf_op | source)
XLA Modules:
  0.0 59.8 jit_solution(11075945176890322127)
XLA Ops:
  0.0 59.0 %shard_map.100 = f32[84,2048]{1,0:T(8,128)S(1)} custom-call(bf16[268,2048]{1,0:T(8,128)(2,1)} %bitcast.8, s32[1,2048]{1,0:T(1,128)} %bitcast.11, s32[32,640]{1,0:T(8,128)} %bitcast.10, bf16[268,512]{1,0:T(8,128)(2,1)} %w_in_hbm.1, f32[1,512]{1,0:T(1,128)} %bitcast.12, f32[1,512]{1,0:T(1,128)} %bitcast.13, bf16[3,512,128]{2,1,0:T(8,128)(2,1)} %wqkv_hbm.1, ...), custom_call_target="tpu_custom_call" | custom-call | flops 10000000000 | bytes 4000000 | tf_op jit(solution)/shard_map/pallas_call | solution.py:362
  59.0 0.9 %copy.12 = f32[2048,84]{0,1:T(8,128)} copy(f32[2048,84]{0,1:T(8,128)S(1)} %bitcast.7) | data formatting | bytes 1376256

commit v5 on v4

--- a/solution.py
+++ b/solution.py
@@ -20,7 +20,6 @@
     *("sr0", "sr1", "sl0", "sl1", "sf0", "sf1"),
     *("su0", "su1", "su2", "su3", "su4", "su5", "su6"),
     *("sd0", "sd1", "sd2", "sd3", "sd4", "sd5", "sd6"),
-    *("xr", "xl", "xo"),
     *("mr0", "mr1", "ml0", "ml1", "mf0", "mf1"),
     *("md0", "md1", "md2", "md3", "md4", "md5", "md6"),
 )
@@ -47,7 +46,7 @@
     x, nbr, w_in, w_in_t, b_t, wqkv, wo, wdec, wdec_t, whead,
     rel, slots, code_hi, code_lo, onehot, embed, e2,
     send_n, recv_n, part, ra, ra_l, ra_r, rb, rb_l, rb_r,
-    st, query, kv, bias, acc, top, norm, mixed, mix_out, md, md_t,
+    st, query, kv, bias, acc, top, norm, mixed, wod, from_state, last_t,
     ssem, rsem, lsem,
 ):
     r = lax.axis_index("region")
@@ -66,7 +65,7 @@
 
     points = x.shape[1]
     width = embed.shape[0]
-    nodes = st.shape[0]
+    nodes = nbr.shape[1]
     quarter = nodes // 4
     half = quarter // 2
     span = 3 * nodes
@@ -127,20 +126,22 @@
     order = (opp_m, right_m, left_m, m)
 
     def rows_of(ref, q, start=0, size=quarter, slot=0):
-        first = slot * nodes + q * quarter + start
-        return ref.at[pl.ds(first if isinstance(first, int) else pl.multiple_of(first, 16), size)]
-
-    def sums(slot, k, count):
-        for i in range(k, k + count):
-            ids = lax.broadcasted_iota(jnp.int32, (quarter, points), 0) + (slot * nodes + order[i] * quarter)
-            rows_of(onehot, i, slot=slot)[...] = (ids == rel[...]).astype(F32).astype(BF16)
-        return nt(rows_of(onehot, k, 0, count * quarter, slot)[...], embed[...])
+        return ref.at[pl.ds(pl.multiple_of(slot * nodes + q * quarter + start, 16), size)]
+
+    def sums(slot, quarters):
+        picks = []
+        for q in quarters:
+            first = slot * nodes + q * quarter
+            ids = lax.broadcasted_iota(jnp.int32, (quarter, points), 0) + first
+            picks.append((ids == rel[...]).astype(F32).astype(BF16))
+            rows_of(onehot, q, slot=slot)[...] = picks[-1]
+        return nt(jnp.concatenate(picks, axis=0), embed[...])
 
     for k in (0, 2):
-        rows_of(send_n, k, 0, 2 * quarter)[...] = sums(1, k, 2).astype(BF16)
+        rows_of(send_n, k, 0, 2 * quarter)[...] = sums(1, order[k:k + 2]).astype(BF16)
         for i in (k, k + 1):
             send("n%d" % i, rows_of(send_n, i), rows_of(recv_n, i), up)
-    part[...] = sums(0, 0, 4)
+    part[...] = sums(0, order)
 
     for i, (name, h) in enumerate((("or", left_m), ("ol", right_m), ("oo", opp_m))):
         arrived(name, wo_half(h, core))
@@ -205,140 +206,124 @@
     mean = jnp.mean(mesh_in * mesh_in, axis=-1, keepdims=True)
     state = (mesh_in * lax.rsqrt(mean + 1e-05) * gain_ref[...]).astype(BF16)
 
-    def share(ref, tag, here_at, there_at, pass_on):
-        def view(at, who, start=0, size=quarter):
-            return rows_of(ref, at[who], start, size)
-
-        def give(name, who, whose, start, dev):
-            send(tag + name, view(here_at, who, start, half), view(there_at(who, whose), whose, start, half), dev)
-
-        def got(name, who, start):
-            arrived(tag + name, view(here_at, who, start, half))
-
-        give("r0", "own", "left", 0, right)
-        give("l1", "own", "right", half, left)
-        pass_on(0, "own", 0, quarter)
-        give("r1", "own", "left", half, right)
-        give("l0", "own", "right", 0, left)
+    def share(view, tag, size, slot, out):
+        cut = size // 2
+
+        def give(name, q, start, dev):
+            send(tag + name, view(slot, q, start, cut), view(slot, q, start, cut), dev)
+
+        def got(name, q, start):
+            arrived(tag + name, view(slot, q, start, cut))
+
+        def pass_on(i, q, start=0, count=cut):
+            for name, to_slot, dev in out:
+                send(name + str(i), view(slot, q, start, count), view(to_slot, q, start, count), dev)
+
+        give("r0", m, 0, right)
+        give("l1", m, cut, left)
+        pass_on(0, m, 0, size)
+        give("r1", m, cut, right)
+        give("l0", m, 0, left)
         yield
-        got("r0", "left", 0)
-        give("f0", "left", "opp", 0, right)
-        pass_on(1, "left", 0, half)
-        got("l1", "right", half)
-        give("f1", "right", "opp", half, left)
-        pass_on(2, "right", half, half)
+        got("r0", left_m, 0)
+        give("f0", left_m, 0, right)
+        pass_on(1, left_m)
+        got("l1", right_m, cut)
+        give("f1", right_m, cut, left)
+        pass_on(2, right_m, cut)
         yield
-        got("r1", "left", half)
-        pass_on(3, "left", half, half)
-        got("l0", "right", 0)
-        pass_on(4, "right", 0, half)
+        got("r1", left_m, cut)
+        pass_on(3, left_m, cut)
+        got("l0", right_m, 0)
+        pass_on(4, right_m)
         yield
-        got("f0", "opp", 0)
-        pass_on(5, "opp", 0, half)
-        got("f1", "opp", half)
-        pass_on(6, "opp", half, half)
+        got("f0", opp_m, 0)
+        pass_on(5, opp_m)
+        got("f1", opp_m, cut)
+        pass_on(6, opp_m, cut)
         yield
 
-    def all_passed(ref, name, slot, shift=0, which=range(7)):
-        for i in which:
-            arrived(name + str(i), rows_of(ref, 0, 0, half if i else quarter, slot), shift)
-
-    own = rows_of(st, m)
-    own[...] = state
-    by_number = {"own": m, "left": left_m, "right": right_m, "opp": opp_m}
-    pieces = []
-    steps = share(st, "s", by_number, lambda who, whose: {whose: by_number[who]}, lambda *piece: pieces.append(piece))
-
-    def project():
-        new = jnp.concatenate([rows_of(st, by_number[who], start, size)[...] for _, who, start, size in pieces], axis=0)
-        qkv = nn(new, wqkv[...])
-        first = 0
-        for i, who, start, size in pieces:
-            rows = qkv[first:first + size]
-            first += size
-            rows_of(query, by_number[who], start, size)[...] = (rows[:, :head_width] * scale).astype(BF16)
-            rows_of(kv, by_number[who], start, size, 1)[...] = rows[:, head_width:].astype(BF16)
-            for name, slot, dev in (("su", 0, up), ("sd", 2, down)):
-                send(name + str(i), rows_of(kv, by_number[who], start, size, 1), rows_of(kv, by_number[who], start, size, slot), dev)
-        pieces.clear()
-
-    scale = LOG2_E * head_width ** -0.5
-    next(steps)
-    for j in range(3):
-        loads["w%d" % j].wait()
-    project()
+    def all_passed(view, name, slot, size, shift=0):
+        for i in range(7):
+            arrived(name + str(i), view(slot, 0, 0, size // 2 if i else size), shift)
+
+    def state_view(slot, q, start, size):
+        return rows_of(st, q, start, size, slot)
+
+    state_view(1, m, 0, quarter)[...] = state
+    steps = share(state_view, "s", quarter, 1, (("su", 0, up), ("sd", 2, down)))
+    next(steps)
     counts(2)
     next(steps)
-    project()
     counts(3)
     next(steps)
-    project()
 
     loads["wdec"].wait()
     wdec_t[...] = jnp.transpose(wdec[...].astype(F32)).astype(BF16)
     e2[...] = nn(wdec_t[...], embed[...])
     next(steps)
-    project()
+
+    scale = LOG2_E * head_width ** -0.5
+    for j in range(3):
+        loads["w%d" % j].wait()
+
+    def project(slot):
+        rows = pl.ds(pl.multiple_of(slot * nodes, 128), nodes)
+        if isinstance(slot, int):
+            query[...] = (nn(st[rows, :], wqkv[:, :head_width]) * scale).astype(BF16)
+        kv[...] = nn(st[rows, :], wqkv[:, head_width:]).astype(BF16)
 
     def attend(slot, first):
-        rows = pl.ds(pl.multiple_of(slot * nodes, 128), nodes)
-        masked = nt(query[...], kv[rows, :head_width]) + bias[:, rows]
+        project(slot)
+        cols = pl.ds(pl.multiple_of(slot * nodes, 128), nodes)
+        masked = nt(query[...], kv[:, :head_width]) + bias[:, cols]
         new = jnp.max(masked, axis=-1, keepdims=True)
         if not first:
             new = jnp.maximum(new, top[...])
             old = jnp.exp2(top[...] - new)
         power = jnp.exp2(masked - new)
         count = jnp.sum(power, axis=-1, keepdims=True)
-        summed = nn(power.astype(BF16), kv[rows, head_width:])
+        summed = nn(power.astype(BF16), kv[:, head_width:])
         norm[...] = count if first else norm[...] * old + count
         acc[...] = summed if first else acc[...] * old + summed
         top[...] = new
 
     shift = INDEX["sd0"] - INDEX["su0"]
     attend(1, True)
-    all_passed(kv, "su", 2 - 2 * core, shift * (1 - core))
+    all_passed(state_view, "su", 2 - 2 * core, quarter, shift * (1 - core))
     attend(2 - 2 * core, False)
-    all_passed(kv, "su", 2 * core, shift * core)
+    all_passed(state_view, "su", 2 * core, quarter, shift * core)
     attend(2 * core, False)
 
-    mix_out[...] = (acc[...] / norm[...]).astype(BF16)
-    mine = pl.ds(pl.multiple_of(m * head_width, 128), head_width)
-    for name, q, dev in (("xr", right_m, right), ("xl", left_m, left), ("xo", opp_m, opposite)):
-        send(name, rows_of(mix_out, q), mixed.at[:, mine], dev)
-    mixed[:, mine] = rows_of(mix_out, m)[...]
+    def mixed_view(slot, h, start, size):
+        cols = pl.ds(pl.multiple_of(h * head_width, 128), head_width)
+        return mixed.at[pl.ds(slot * nodes + start, size), cols]
+
+    mixed_view(0, m, 0, nodes)[...] = (acc[...] / norm[...]).astype(BF16)
+    steps = share(mixed_view, "m", nodes, 0, (("md", 1, down),))
+    next(steps)
+
     loads["wo"].wait()
     for i, h in enumerate((left_m, right_m, opp_m)):
         arrived("os%d" % i, wo_half(h, 1 - core))
-    for name in ("xr", "xl", "xo"):
-        arrived(name, mixed.at[:, mine])
-    attended = nn(mixed[...], wo[...].reshape(heads * head_width, width))
-    mesh_out = (own[...].astype(F32) + attended).astype(BF16)
-    rows_of(md, 3)[...] = nn(mesh_out, wdec[...]).astype(BF16)
-
-    by_place = {"own": 3, "left": 2, "right": 1, "opp": 0}
-
-    def to_the_region_before(i, who, start, size):
-        at = by_place[who]
-        send("md%d" % i, rows_of(md, at, start, size), rows_of(md, at, start, size, 1), down)
-
-    for _ in share(md, "m", by_place, lambda who, whose: by_place, to_the_region_before):
-        pass
-
-    def turned(first, count):
-        return jnp.transpose(md[pl.ds(first, count), :].astype(F32)).astype(BF16)
-
-    e2[...] += nn(turned(0, nodes), onehot[pl.ds(0, nodes), :])
+    wod[...] = nn(wo[...].reshape(heads * head_width, width), wdec[...]).astype(BF16)
+    next(steps)
+    from_state[...] = nn(st[nodes:, :], wdec[...])
+    next(steps)
+    next(steps)
+
+    def decoded(slot):
+        rows = pl.ds(slot * nodes, nodes)
+        return jnp.transpose(nn(mixed[rows, :], wod[...]) + from_state[rows, :]).astype(BF16)
+
+    e2[...] += nn(decoded(0), onehot[pl.ds(0, nodes), :])
     loads["whead"].wait()
-    all_passed(md, "md", 1, which=range(5))
-    late = -(-quarter // 128) * 128
-    if late < nodes:
-        e2[...] += nn(turned(nodes + late, nodes - late), onehot[pl.ds(nodes + late, nodes - late), :])
-    all_passed(md, "md", 1, which=(5, 6))
-    md_t[...] = turned(nodes, late)
+    all_passed(mixed_view, "md", 1, nodes)
+    last_t[...] = decoded(1)
     block = min(1024, points)
     for i in range(points // block):
         cols = slice(i * block, (i + 1) * block)
-        z = e2[:, cols] + nn(md_t[...], onehot[nodes:nodes + late, cols])
+        z = e2[:, cols] + nn(last_t[...], onehot[nodes:, cols])
         out_ref[:, cols] = nn(whead[...], silu(z).astype(BF16))
 
     for c in started:
@@ -375,10 +360,10 @@
             V((nodes, width), BF16), V((nodes, width), BF16), V((nodes, width), F32),
             V((quarter, width), BF16), V((half, width), BF16), V((half, width), BF16),
             V((2, quarter, width), BF16), V((quarter, width), BF16), V((quarter, width), BF16),
-            V((nodes, width), BF16), V((nodes, head_width), BF16), V((span, 2 * head_width), BF16),
+            V((span, width), BF16), V((nodes, head_width), BF16), V((nodes, 2 * head_width), BF16),
             V((nodes, span), F32), V((nodes, head_width), F32), V((nodes, 1), F32), V((nodes, 1), F32),
-            V((quarter, heads * head_width), BF16), V((nodes, head_width), BF16),
-            V((2 * nodes, width), BF16), V((width, -(-quarter // 128) * 128), BF16),
+            V((2 * nodes, heads * head_width), BF16), V((heads * head_width, width), BF16),
+            V((2 * nodes, width), F32), V((width, nodes), BF16),
             pltpu.SemaphoreType.DMA((len(NAMES),)), pltpu.SemaphoreType.DMA((len(NAMES),)),
             pltpu.SemaphoreType.DMA((9,)),
         ],

time: 60 us -> 55.9 us (0.932); the launches traced: 59.8 us -> 54.8 us
  Pallas kernels: 59 us -> 53.9 us
    pallas_call x1, Pallas kernels: 59 us -> 53.9 us  [on_device(): pl.pallas_call(functools.partial(kernel, regions), out_shape=pltpu.VMEM((...]
where the time goes in v5:
time: 55.9 us; the launch traced here: 54.8 us
  Pallas kernels  53.9 us (96%)
  local copies, waits for them, and re-layouts  0.86 us (2%)
    pallas_call x1, Pallas kernels, on_device(): pl.pallas_call(functools.partial(kernel, regions), out_shape=pltpu.VMEM((...  53.9 us

profile of v5, /device:TPU:2, one launch (start us, length us, event | category | flops | bytes accessed | tf_op | source)
XLA Modules:
  0.0 54.8 jit_solution(5500501268247153636)
XLA Ops:
  0.0 53.9 %shard_map.100 = f32[84,2048]{1,0:T(8,128)S(1)} custom-call(bf16[268,2048]{1,0:T(8,128)(2,1)} %bitcast.8, s32[1,2048]{1,0:T(1,128)} %bitcast.11, s32[32,640]{1,0:T(8,128)} %bitcast.10, bf16[268,512]{1,0:T(8,128)(2,1)} %w_in_hbm.1, f32[1,512]{1,0:T(1,128)} %bitcast.12, f32[1,512]{1,0:T(1,128)} %bitcast.13, bf16[3,512,128]{2,1,0:T(8,128)(2,1)} %wqkv_hbm.1, ...), custom_call_target="tpu_custom_call" | custom-call | flops 10000000000 | bytes 4000000 | tf_op jit(solution)/shard_map/pallas_call | solution.py:347
  53.9 0.9 %copy.12 = f32[2048,84]{0,1:T(8,128)} copy(f32[2048,84]{0,1:T(8,128)S(1)} %bitcast.7) | data formatting | bytes 1376256

commit v6 on v5

--- a/solution.py
+++ b/solution.py
@@ -17,11 +17,11 @@
     *("or", "ol", "oo", "os0", "os1", "os2"),
     *("n0", "n1", "n2", "n3"),
     *("ar", "al", "br0", "br1", "bl0", "bl1"),
-    *("sr0", "sr1", "sl0", "sl1", "sf0", "sf1"),
-    *("su0", "su1", "su2", "su3", "su4", "su5", "su6"),
-    *("sd0", "sd1", "sd2", "sd3", "sd4", "sd5", "sd6"),
-    *("mr0", "mr1", "ml0", "ml1", "mf0", "mf1"),
-    *("md0", "md1", "md2", "md3", "md4", "md5", "md6"),
+    *("sr0", "sr1", "sr2", "sl0", "sl1", "sl2", "sf0", "sf1", "sg0", "sg1"),
+    *("su%d" % i for i in range(11)),
+    *("sd%d" % i for i in range(11)),
+    *("mr0", "mr1", "mr2", "ml0", "ml1", "ml2", "mf0", "mf1", "mg0", "mg1"),
+    *("md%d" % i for i in range(11)),
 )
 INDEX = {name: i for i, name in enumerate(NAMES)}
 
@@ -193,12 +193,14 @@
     arrived("ar", ra_l)
     rb[0, lo] = (both(1, 0, half) + ra_l[...].astype(F32)).astype(BF16)
     send("br0", rb.at[0, lo], rb_l.at[lo], right)
+    counts(2)
     arrived("n2", rows_of(recv_n, 2))
     rb[1, lo] = both(2, 0, half).astype(BF16)
     send("bl0", rb.at[1, lo], rb_r.at[lo], left)
     arrived("al", ra_r)
     rb[1, hi] = (both(2, half, half) + ra_r[...].astype(F32)).astype(BF16)
     send("bl1", rb.at[1, hi], rb_r.at[hi], left)
+    counts(3)
     arrived("n3", rows_of(recv_n, 3))
     for name, ref in (("br1", rb_l.at[hi]), ("br0", rb_l.at[lo]), ("bl0", rb_r.at[lo]), ("bl1", rb_r.at[hi])):
         arrived(name, ref)
@@ -206,46 +208,55 @@
     mean = jnp.mean(mesh_in * mesh_in, axis=-1, keepdims=True)
     state = (mesh_in * lax.rsqrt(mean + 1e-05) * gain_ref[...]).astype(BF16)
 
+    def share_pieces(size):
+        cut = size // 2
+        one = -(-cut // 32) * 16
+        return {"0": (0, one), "1": (one, cut - one), "2": (cut, cut)}, {"0": (cut, one), "1": (cut + one, cut - one), "2": (0, cut)}
+
     def share(view, tag, size, slot, out):
-        cut = size // 2
-
-        def give(name, q, start, dev):
-            send(tag + name, view(slot, q, start, cut), view(slot, q, start, cut), dev)
-
-        def got(name, q, start):
-            arrived(tag + name, view(slot, q, start, cut))
-
-        def pass_on(i, q, start=0, count=cut):
+        to_right, to_left = share_pieces(size)
+
+        def give(name, q, piece, dev):
+            send(tag + name, view(slot, q, *piece), view(slot, q, *piece), dev)
+
+        def got(name, q, piece):
+            arrived(tag + name, view(slot, q, *piece))
+
+        def pass_on(i, q, piece):
             for name, to_slot, dev in out:
-                send(name + str(i), view(slot, q, start, count), view(to_slot, q, start, count), dev)
-
-        give("r0", m, 0, right)
-        give("l1", m, cut, left)
-        pass_on(0, m, 0, size)
-        give("r1", m, cut, right)
-        give("l0", m, 0, left)
+                send(name + str(i), view(slot, q, *piece), view(to_slot, q, *piece), dev)
+
+        give("r0", m, to_right["0"], right)
+        give("l0", m, to_left["0"], left)
+        pass_on(0, m, (0, size))
+        for k in ("1", "2"):
+            give("r" + k, m, to_right[k], right)
+            give("l" + k, m, to_left[k], left)
         yield
-        got("r0", left_m, 0)
-        give("f0", left_m, 0, right)
-        pass_on(1, left_m)
-        got("l1", right_m, cut)
-        give("f1", right_m, cut, left)
-        pass_on(2, right_m, cut)
+        for i, k in ((1, "0"), (3, "1")):
+            got("r" + k, left_m, to_right[k])
+            give("f" + k, left_m, to_right[k], right)
+            pass_on(i, left_m, to_right[k])
+            got("l" + k, right_m, to_left[k])
+            give("g" + k, right_m, to_left[k], left)
+            pass_on(i + 1, right_m, to_left[k])
         yield
-        got("r1", left_m, cut)
-        pass_on(3, left_m, cut)
-        got("l0", right_m, 0)
-        pass_on(4, right_m)
+        got("r2", left_m, to_right["2"])
+        pass_on(5, left_m, to_right["2"])
+        got("l2", right_m, to_left["2"])
+        pass_on(6, right_m, to_left["2"])
         yield
-        got("f0", opp_m, 0)
-        pass_on(5, opp_m)
-        got("f1", opp_m, cut)
-        pass_on(6, opp_m, cut)
+        for i, k in ((7, "0"), (9, "1")):
+            got("f" + k, opp_m, to_right[k])
+            pass_on(i, opp_m, to_right[k])
+            got("g" + k, opp_m, to_left[k])
+            pass_on(i + 1, opp_m, to_left[k])
         yield
 
     def all_passed(view, name, slot, size, shift=0):
-        for i in range(7):
-            arrived(name + str(i), view(slot, 0, 0, size // 2 if i else size), shift)
+        pieces = share_pieces(size)[0]
+        for i, k in enumerate((None, "0", "0", "1", "1", "2", "2", "0", "0", "1", "1")):
+            arrived(name + str(i), view(slot, 0, 0, pieces[k][1] if k else size), shift)
 
     def state_view(slot, q, start, size):
         return rows_of(st, q, start, size, slot)
@@ -253,9 +264,7 @@
     state_view(1, m, 0, quarter)[...] = state
     steps = share(state_view, "s", quarter, 1, (("su", 0, up), ("sd", 2, down)))
     next(steps)
-    counts(2)
-    next(steps)
-    counts(3)
+    next(steps)
     next(steps)
 
     loads["wdec"].wait()

time: 55.9 us -> 56.3 us (level)
  Pallas kernels: 53.9 us -> 54.8 us
    pallas_call x1, Pallas kernels: 53.9 us -> 54.8 us  [on_device(): pl.pallas_call(functools.partial(kernel, regions), out_shape=pltpu.VMEM((...]
where the time goes in v6:
time: 56.3 us; the launch traced here: 55.7 us
  Pallas kernels  54.8 us (97%)
  local copies, waits for them, and re-layouts  0.86 us (2%)
    pallas_call x1, Pallas kernels, on_device(): pl.pallas_call(functools.partial(kernel, regions), out_shape=pltpu.VMEM((...  54.8 us

profile of v6, /device:TPU:2, one launch (start us, length us, event | category | flops | bytes accessed | tf_op | source)
XLA Modules:
  0.0 55.7 jit_solution(12223437717823271795)
XLA Ops:
  0.0 54.8 %shard_map.100 = f32[84,2048]{1,0:T(8,128)S(1)} custom-call(bf16[268,2048]{1,0:T(8,128)(2,1)} %bitcast.8, s32[1,2048]{1,0:T(1,128)} %bitcast.11, s32[32,640]{1,0:T(8,128)} %bitcast.10, bf16[268,512]{1,0:T(8,128)(2,1)} %w_in_hbm.1, f32[1,512]{1,0:T(1,128)} %bitcast.12, f32[1,512]{1,0:T(1,128)} %bitcast.13, bf16[3,512,128]{2,1,0:T(8,128)(2,1)} %wqkv_hbm.1, ...), custom_call_target="tpu_custom_call" | custom-call | flops 10000000000 | bytes 4000000 | tf_op jit(solution)/shard_map/pallas_call | solution.py:356
  54.8 0.9 %copy.12 = f32[2048,84]{0,1:T(8,128)} copy(f32[2048,84]{0,1:T(8,128)S(1)} %bitcast.7) | data formatting | bytes 1376256

commit v7 on v5

--- a/solution.py
+++ b/solution.py
@@ -41,9 +41,9 @@
 
 def kernel(
     regions,
-    x_hbm, targets_ref, nbr_hbm, w_in_hbm, b_ref, gain_ref, wqkv_hbm, wo_hbm, wdec_hbm, whead_hbm,
+    x_hbm, targets_hbm, nbr_hbm, w_in_hbm, b_hbm, gain_hbm, wqkv_hbm, wo_hbm, wdec_hbm, whead_hbm,
     out_ref,
-    x, nbr, w_in, w_in_t, b_t, wqkv, wo, wdec, wdec_t, whead,
+    x, targets, nbr, w_in, b_in, gain, w_in_t, b_t, wqkv, wo, wdec, wdec_t, whead,
     rel, slots, code_hi, code_lo, onehot, embed, e2,
     send_n, recv_n, part, ra, ra_l, ra_r, rb, rb_l, rb_r,
     st, query, kv, bias, acc, top, norm, mixed, wod, from_state, last_t,
@@ -74,8 +74,8 @@
 
     started = []
 
-    def send(name, src, dst, dev):
-        i = INDEX[name]
+    def send(name, src, dst, dev, shift=0):
+        i = INDEX[name] + shift
         c = pltpu.make_async_remote_copy(
             src_ref=src, dst_ref=dst, send_sem=ssem.at[i], recv_sem=rsem.at[i],
             device_id=dev, device_id_type=MESH,
@@ -83,6 +83,11 @@
         c.start()
         started.append(c)
 
+    def sent():
+        for c in started:
+            c.wait_send()
+        started.clear()
+
     def arrived(name, dst, shift=0):
         i = INDEX[name] + shift
         pltpu.make_async_remote_copy(
@@ -92,7 +97,7 @@
 
     loads = {}
     for i, (name, src, dst) in enumerate((
-        ("w_in", w_in_hbm, w_in), ("x", x_hbm, x), ("wo", wo_hbm, wo.at[m]), ("wdec", wdec_hbm, wdec), ("whead", whead_hbm, whead), ("nbr", nbr_hbm, nbr),
+        ("w_in", w_in_hbm, w_in), ("x", x_hbm, x), ("b", b_hbm, b_in), ("targets", targets_hbm, targets), ("gain", gain_hbm, gain), ("wo", wo_hbm, wo.at[m]), ("wdec", wdec_hbm, wdec), ("whead", whead_hbm, whead), ("nbr", nbr_hbm, nbr),
         *(("w%d" % j, wqkv_hbm.at[j], wqkv.at[:, pl.ds(j * head_width, head_width)]) for j in range(3)),
     )):
         loads[name] = pltpu.make_async_copy(src, dst, lsem.at[i])
@@ -104,24 +109,27 @@
 
     here = r * nodes
     total = regions * nodes
-    t = targets_ref[...] - here
-    rel[...] = jnp.where(t < 0, t + total, t)
-    b_t[...] = jnp.transpose(jnp.broadcast_to(b_ref[...], (128, width)))
-    pl.semaphore_wait(barrier, 5)
-
-    ho = head_width // 2
-
-    def wo_half(h, which):
-        return wo.at[h, pl.ds(pl.multiple_of(which * ho, 16), ho), :]
-
-    for name, dev in (("or", right), ("ol", left), ("oo", opposite)):
-        send(name, wo_hbm.at[pl.ds(pl.multiple_of(core * ho, 16), ho), :], wo_half(m, core), dev)
-
     loads["w_in"].wait()
     w_in_t[...] = jnp.transpose(w_in[...].astype(F32)).astype(BF16)
+    loads["b"].wait()
+    b_t[...] = jnp.transpose(jnp.broadcast_to(b_in[...], (128, width)))
+    loads["targets"].wait()
+    t = targets[...] - here
+    rel[...] = jnp.where(t < 0, t + total, t)
+
     loads["x"].wait()
     z = nn(w_in_t[...], x[...]) + jnp.concatenate([b_t[...]] * (points // 128), axis=1)
     embed[...] = silu(z).astype(BF16)
+
+    pl.semaphore_wait(barrier, 5)
+
+    ho = head_width // 2
+
+    def wo_half(h, which):
+        return wo.at[h, pl.ds(pl.multiple_of(which * ho, 16), ho), :]
+
+    for name, dev in (("or", right), ("ol", left), ("oo", opposite)):
+        send(name, wo_hbm.at[pl.ds(pl.multiple_of(core * ho, 16), ho), :], wo_half(m, core), dev)
 
     order = (opp_m, right_m, left_m, m)
 
@@ -184,8 +192,6 @@
     def counts(i):
         lax.fori_loop(i * share_of_counts, (i + 1) * share_of_counts, count_groups, 0)
 
-    counts(0)
-    counts(1)
 
     arrived("n1", rows_of(recv_n, 1))
     rb[0, hi] = both(1, half, half).astype(BF16)
@@ -203,8 +209,9 @@
     for name, ref in (("br1", rb_l.at[hi]), ("br0", rb_l.at[lo]), ("bl0", rb_r.at[lo]), ("bl1", rb_r.at[hi])):
         arrived(name, ref)
     mesh_in = both(3) + rb_l[...].astype(F32) + rb_r[...].astype(F32)
+    loads["gain"].wait()
     mean = jnp.mean(mesh_in * mesh_in, axis=-1, keepdims=True)
-    state = (mesh_in * lax.rsqrt(mean + 1e-05) * gain_ref[...]).astype(BF16)
+    state = (mesh_in * lax.rsqrt(mean + 1e-05) * gain[...]).astype(BF16)
 
     def share(view, tag, size, slot, out):
         cut = size // 2
@@ -216,8 +223,8 @@
             arrived(tag + name, view(slot, q, start, cut))
 
         def pass_on(i, q, start=0, count=cut):
-            for name, to_slot, dev in out:
-                send(name + str(i), view(slot, q, start, count), view(to_slot, q, start, count), dev)
+            for name, to_slot, dev, shift in out:
+                send(name + str(i), view(slot, q, start, count), view(to_slot, q, start, count), dev, shift)
 
         give("r0", m, 0, right)
         give("l1", m, cut, left)
@@ -250,17 +257,19 @@
     def state_view(slot, q, start, size):
         return rows_of(st, q, start, size, slot)
 
+    shift = INDEX["sd0"] - INDEX["su0"]
+    far = "su", 2 - 2 * core, (lax.rem(r + regions - 1 + 2 * core, regions), m)
+    near = "su", 2 * core, sibling
     state_view(1, m, 0, quarter)[...] = state
-    steps = share(state_view, "s", quarter, 1, (("su", 0, up), ("sd", 2, down)))
+    steps = share(state_view, "s", quarter, 1, ((*far, shift * (1 - core)), (*near, shift * core)))
+    next(steps)
+    counts(0)
+    counts(1)
     next(steps)
     counts(2)
     next(steps)
     counts(3)
-    next(steps)
-
-    loads["wdec"].wait()
-    wdec_t[...] = jnp.transpose(wdec[...].astype(F32)).astype(BF16)
-    e2[...] = nn(wdec_t[...], embed[...])
+
     next(steps)
 
     scale = LOG2_E * head_width ** -0.5
@@ -288,7 +297,6 @@
         acc[...] = summed if first else acc[...] * old + summed
         top[...] = new
 
-    shift = INDEX["sd0"] - INDEX["su0"]
     attend(1, True)
     all_passed(state_view, "su", 2 - 2 * core, quarter, shift * (1 - core))
     attend(2 - 2 * core, False)
@@ -300,15 +308,19 @@
         return mixed.at[pl.ds(slot * nodes + start, size), cols]
 
     mixed_view(0, m, 0, nodes)[...] = (acc[...] / norm[...]).astype(BF16)
-    steps = share(mixed_view, "m", nodes, 0, (("md", 1, down),))
+    steps = share(mixed_view, "m", nodes, 0, (("md", 1, down, 0),))
     next(steps)
 
     loads["wo"].wait()
     for i, h in enumerate((left_m, right_m, opp_m)):
         arrived("os%d" % i, wo_half(h, 1 - core))
+    loads["wdec"].wait()
     wod[...] = nn(wo[...].reshape(heads * head_width, width), wdec[...]).astype(BF16)
-    next(steps)
     from_state[...] = nn(st[nodes:, :], wdec[...])
+
+    wdec_t[...] = jnp.transpose(wdec[...].astype(F32)).astype(BF16)
+    e2[...] = nn(wdec_t[...], embed[...])
+    next(steps)
     next(steps)
     next(steps)
 
@@ -318,16 +330,16 @@
 
     e2[...] += nn(decoded(0), onehot[pl.ds(0, nodes), :])
     loads["whead"].wait()
+    sent()
     all_passed(mixed_view, "md", 1, nodes)
     last_t[...] = decoded(1)
-    block = min(1024, points)
+    block = points
     for i in range(points // block):
         cols = slice(i * block, (i + 1) * block)
         z = e2[:, cols] + nn(last_t[...], onehot[nodes:, cols])
         out_ref[:, cols] = nn(whead[...], silu(z).astype(BF16))
 
-    for c in started:
-        c.wait_send()
+    sent()
 
 
 def on_device(grid_state, targets, neighbours, w_in, b_in, mesh_gain, w_qkv, w_out, w_dec, w_head):
@@ -347,10 +359,11 @@
     out = pl.pallas_call(
         functools.partial(kernel, regions),
         out_shape=pltpu.VMEM((out_width, points), F32),
-        in_specs=[anyw, vmem, anyw, anyw, vmem, vmem, anyw, anyw, anyw, anyw],
+        in_specs=[anyw] * 10,
         out_specs=vmem,
         scratch_shapes=[
-            V((channels, points), BF16), V((nbr, nodes), jnp.int32), V((channels, width), BF16),
+            V((channels, points), BF16), V((1, points), jnp.int32), V((nbr, nodes), jnp.int32), V((channels, width), BF16),
+            V((1, width), F32), V((1, width), F32),
             V((width, channels), BF16), V((width, 128), F32), V((width, 3 * head_width), BF16),
             V((heads, head_width, width), BF16), V((width, width), BF16), V((width, width), BF16),
             V((out_width, width), BF16),
@@ -365,7 +378,7 @@
             V((2 * nodes, heads * head_width), BF16), V((heads * head_width, width), BF16),
             V((2 * nodes, width), F32), V((width, nodes), BF16),
             pltpu.SemaphoreType.DMA((len(NAMES),)), pltpu.SemaphoreType.DMA((len(NAMES),)),
-            pltpu.SemaphoreType.DMA((9,)),
+            pltpu.SemaphoreType.DMA((12,)),
         ],
         compiler_params=pltpu.CompilerParams(
             collective_id=0, has_side_effects=True, vmem_limit_bytes=56 * 1024 * 1024

time: 55.9 us -> 53.2 us (0.952); the launches traced: 54.8 us -> 53.1 us
  Pallas kernels: 53.9 us -> 52.3 us
    pallas_call x1, Pallas kernels: 53.9 us -> 52.3 us  [on_device(): pl.pallas_call(functools.partial(kernel, regions), out_shape=pltpu.VMEM((...]
where the time goes in v7:
time: 53.2 us; the launch traced here: 53.1 us
  Pallas kernels  52.3 us (98%)
  local copies, waits for them, and re-layouts  0.86 us (2%)
    pallas_call x1, Pallas kernels, on_device(): pl.pallas_call(functools.partial(kernel, regions), out_shape=pltpu.VMEM((...  52.3 us

profile of v7, /device:TPU:2, one launch (start us, length us, event | category | flops | bytes accessed | tf_op | source)
XLA Modules:
  0.0 53.1 jit_solution(12099661415211204277)
XLA Ops:
  0.0 52.3 %shard_map.100 = f32[84,2048]{1,0:T(8,128)S(1)} custom-call(bf16[268,2048]{1,0:T(8,128)(2,1)} %bitcast.8, s32[1,2048]{1,0:T(1,128)} %bitcast.11, s32[32,640]{1,0:T(8,128)} %bitcast.10, bf16[268,512]{1,0:T(8,128)(2,1)} %w_in_hbm.1, f32[1,512]{1,0:T(1,128)} %bitcast.12, f32[1,512]{1,0:T(1,128)} %bitcast.13, bf16[3,512,128]{2,1,0:T(8,128)(2,1)} %wqkv_hbm.1, ...), custom_call_target="tpu_custom_call" | custom-call | flops 10000000000 | bytes 4000000 | tf_op jit(solution)/shard_map/pallas_call | solution.py:359
  52.3 0.9 %copy.12 = f32[2048,84]{0,1:T(8,128)} copy(f32[2048,84]{0,1:T(8,128)S(1)} %bitcast.7) | data formatting | bytes 1376256

commit v8 on v7

--- a/solution.py
+++ b/solution.py
@@ -151,10 +151,6 @@
             send("n%d" % i, rows_of(send_n, i), rows_of(recv_n, i), up)
     part[...] = sums(0, order)
 
-    for i, (name, h) in enumerate((("or", left_m), ("ol", right_m), ("oo", opp_m))):
-        arrived(name, wo_half(h, core))
-        send("os%d" % i, wo_half(h, core), wo_half(h, core), sibling)
-
     def both(q, start=0, size=quarter):
         return rows_of(part, q, start, size)[...] + rows_of(recv_n, q, start, size)[...].astype(F32)
 
@@ -193,6 +189,7 @@
         lax.fori_loop(i * share_of_counts, (i + 1) * share_of_counts, count_groups, 0)
 
 
+    counts(0)
     arrived("n1", rows_of(recv_n, 1))
     rb[0, hi] = both(1, half, half).astype(BF16)
     send("br1", rb.at[0, hi], rb_l.at[hi], right)
@@ -263,12 +260,14 @@
     state_view(1, m, 0, quarter)[...] = state
     steps = share(state_view, "s", quarter, 1, ((*far, shift * (1 - core)), (*near, shift * core)))
     next(steps)
-    counts(0)
+    for i, (name, h) in enumerate((("or", left_m), ("ol", right_m), ("oo", opp_m))):
+        arrived(name, wo_half(h, core))
+        send("os%d" % i, wo_half(h, core), wo_half(h, core), sibling)
     counts(1)
-    next(steps)
     counts(2)
     next(steps)
     counts(3)
+    next(steps)
 
     next(steps)
 

time: 53.2 us -> 53.3 us (level)
  no operation moved by 1% of the time
where the time goes in v8:
time: 53.3 us; the launch traced here: 53.2 us
  Pallas kernels  52.3 us (98%)
  local copies, waits for them, and re-layouts  0.86 us (2%)
    pallas_call x1, Pallas kernels, on_device(): pl.pallas_call(functools.partial(kernel, regions), out_shape=pltpu.VMEM((...  52.3 us

profile of v8, /device:TPU:2, one launch (start us, length us, event | category | flops | bytes accessed | tf_op | source)
XLA Modules:
  0.0 53.2 jit_solution(13471073713329427351)
XLA Ops:
  0.0 52.3 %shard_map.100 = f32[84,2048]{1,0:T(8,128)S(1)} custom-call(bf16[268,2048]{1,0:T(8,128)(2,1)} %bitcast.8, s32[1,2048]{1,0:T(1,128)} %bitcast.11, s32[32,640]{1,0:T(8,128)} %bitcast.10, bf16[268,512]{1,0:T(8,128)(2,1)} %w_in_hbm.1, f32[1,512]{1,0:T(1,128)} %bitcast.12, f32[1,512]{1,0:T(1,128)} %bitcast.13, bf16[3,512,128]{2,1,0:T(8,128)(2,1)} %wqkv_hbm.1, ...), custom_call_target="tpu_custom_call" | custom-call | flops 10000000000 | bytes 4000000 | tf_op jit(solution)/shard_map/pallas_call | solution.py:358
  52.3 0.9 %copy.12 = f32[2048,84]{0,1:T(8,128)} copy(f32[2048,84]{0,1:T(8,128)S(1)} %bitcast.7) | data formatting | bytes 1376256

commit v9 on v8

--- a/solution.py
+++ b/solution.py
@@ -224,6 +224,7 @@
                 send(name + str(i), view(slot, q, start, count), view(to_slot, q, start, count), dev, shift)
 
         give("r0", m, 0, right)
+        yield
         give("l1", m, cut, left)
         pass_on(0, m, 0, size)
         give("r1", m, cut, right)
@@ -260,6 +261,7 @@
     state_view(1, m, 0, quarter)[...] = state
     steps = share(state_view, "s", quarter, 1, ((*far, shift * (1 - core)), (*near, shift * core)))
     next(steps)
+    next(steps)
     for i, (name, h) in enumerate((("or", left_m), ("ol", right_m), ("oo", opp_m))):
         arrived(name, wo_half(h, core))
         send("os%d" % i, wo_half(h, core), wo_half(h, core), sibling)
@@ -281,34 +283,37 @@
             query[...] = (nn(st[rows, :], wqkv[:, :head_width]) * scale).astype(BF16)
         kv[...] = nn(st[rows, :], wqkv[:, head_width:]).astype(BF16)
 
-    def attend(slot, first):
-        project(slot)
+    def attend(slot, first, at=slice(None), projected=False):
+        if not projected:
+            project(slot)
         cols = pl.ds(pl.multiple_of(slot * nodes, 128), nodes)
-        masked = nt(query[...], kv[:, :head_width]) + bias[:, cols]
+        masked = nt(query[at], kv[:, :head_width]) + bias[at, cols]
         new = jnp.max(masked, axis=-1, keepdims=True)
         if not first:
-            new = jnp.maximum(new, top[...])
-            old = jnp.exp2(top[...] - new)
+            new = jnp.maximum(new, top[at])
+            old = jnp.exp2(top[at] - new)
         power = jnp.exp2(masked - new)
         count = jnp.sum(power, axis=-1, keepdims=True)
         summed = nn(power.astype(BF16), kv[:, head_width:])
-        norm[...] = count if first else norm[...] * old + count
-        acc[...] = summed if first else acc[...] * old + summed
-        top[...] = new
+        norm[at] = count if first else norm[at] * old + count
+        acc[at] = summed if first else acc[at] * old + summed
+        top[at] = new
 
     attend(1, True)
     all_passed(state_view, "su", 2 - 2 * core, quarter, shift * (1 - core))
     attend(2 - 2 * core, False)
     all_passed(state_view, "su", 2 * core, quarter, shift * core)
-    attend(2 * core, False)
 
     def mixed_view(slot, h, start, size):
         cols = pl.ds(pl.multiple_of(h * head_width, 128), head_width)
         return mixed.at[pl.ds(slot * nodes + start, size), cols]
 
-    mixed_view(0, m, 0, nodes)[...] = (acc[...] / norm[...]).astype(BF16)
     steps = share(mixed_view, "m", nodes, 0, (("md", 1, down, 0),))
-    next(steps)
+    for first in (0, nodes // 2):
+        at = slice(first, first + nodes // 2)
+        attend(2 * core, False, at, first > 0)
+        mixed_view(0, m, first, nodes // 2)[...] = (acc[at] / norm[at]).astype(BF16)
+        next(steps)
 
     loads["wo"].wait()
     for i, h in enumerate((left_m, right_m, opp_m)):

time: 53.3 us -> 52.9 us (level)
  no operation moved by 1% of the time
where the time goes in v9:
time: 52.9 us; the launch traced here: 52.8 us
  Pallas kernels  51.9 us (98%)
  local copies, waits for them, and re-layouts  0.86 us (2%)
    pallas_call x1, Pallas kernels, on_device(): pl.pallas_call(functools.partial(kernel, regions), out_shape=pltpu.VMEM((...  51.9 us

profile of v9, /device:TPU:2, one launch (start us, length us, event | category | flops | bytes accessed | tf_op | source)
XLA Modules:
  0.0 52.8 jit_solution(13363693802503443115)
XLA Ops:
  0.0 51.9 %shard_map.100 = f32[84,2048]{1,0:T(8,128)S(1)} custom-call(bf16[268,2048]{1,0:T(8,128)(2,1)} %bitcast.8, s32[1,2048]{1,0:T(1,128)} %bitcast.11, s32[32,640]{1,0:T(8,128)} %bitcast.10, bf16[268,512]{1,0:T(8,128)(2,1)} %w_in_hbm.1, f32[1,512]{1,0:T(1,128)} %bitcast.12, f32[1,512]{1,0:T(1,128)} %bitcast.13, bf16[3,512,128]{2,1,0:T(8,128)(2,1)} %wqkv_hbm.1, ...), custom_call_target="tpu_custom_call" | custom-call | flops 10000000000 | bytes 4000000 | tf_op jit(solution)/shard_map/pallas_call | solution.py:363
  51.9 0.9 %copy.12 = f32[2048,84]{0,1:T(8,128)} copy(f32[2048,84]{0,1:T(8,128)S(1)} %bitcast.7) | data formatting | bytes 1376256
